TPU v7x, 512 devices: a whole 4x8x8 slice. The times are simulated.
512 devices in a mesh: pair: 128 (over z, y, core), blk: 4 (over x).
Axes of the slice: x: 4, y: 8, z: 8, core: 2. Of those that a mesh axis runs over, the one named last changes fastest.
Arguments:
- amplitudes: float32 [512, 16384], P('pair', 'blk'), may hold values from -6 to 6
- virt_ints: float32 [16384, 16384], P('blk', 'pair'), may hold values from -0.09375 to 0.09375
- virt_mask: int32 [128, 128], replicated, may hold values from 0 to 1, as said below
- hole_ints: float32 [512, 512], P('blk'), may hold values from -0.5 to 0.5
- hole_mask: int32 [4, 4], replicated, may hold values from 0 to 1, as said below
Outputs:
- residual: float32 [512, 16384], P('blk', 'pair')
Inputs may be any that keep to these rules, and one draw needn't show every extreme that they name: `virt_mask`: split the 128 block rows into four equal groups in order; in every block column, each group holds exactly 8 ones. `hole_mask`: every block column holds exactly one 1.
All inputs are finite; a program needn't handle non-finite values.
Results may differ from a plain program's by a relative error of at most 0.000057.
Values sent between devices are 32-bit elements; how exact they have to be, the bound alone decides.
No kernel may reach another device: no remote copies, remote signals or barrier semaphores. Data moves between devices by JAX's collectives and lax.ppermute only.
A program may use at most 64 MiB of HBM per device.

v0:
```python
import jax
import jax.numpy as jnp
from jax import lax
from jax.sharding import PartitionSpec as P

BS = 128


PRECISE = lax.Precision.HIGHEST


def block_pick(first, count, total_blocks):
    entry_ids = first + jnp.arange(count, dtype=jnp.int32)
    block_ids = jnp.arange(total_blocks, dtype=jnp.int32)
    return (entry_ids[:, None] // BS == block_ids[None, :]).astype(jnp.float32)


def local_mask(mask, row_first, row_count, col_first, col_count):
    total_blocks = mask.shape[0]
    rows_pick = block_pick(row_first, row_count, total_blocks)
    cols_pick = block_pick(col_first, col_count, total_blocks)
    inner = jnp.dot(mask.astype(jnp.float32), cols_pick.T, precision=PRECISE)
    return jnp.dot(rows_pick, inner, precision=PRECISE)


def per_device(amplitudes, virt_ints, virt_mask, hole_ints, hole_mask):
    pair_index = lax.axis_index("pair")
    blk_index = lax.axis_index("blk")
    pair_count = lax.axis_size("pair")
    local_rows, quarter = amplitudes.shape
    slab_width = virt_ints.shape[1]
    occupied = local_rows * pair_count
    virt_eff = virt_ints * local_mask(
        virt_mask, blk_index * quarter, quarter, pair_index * slab_width, slab_width
    )
    product = jnp.dot(
        lax.all_gather(amplitudes, "pair", axis=0, tiled=True), virt_eff, precision=PRECISE
    )
    particle = lax.psum_scatter(product, "blk", scatter_dimension=0, tiled=True)
    whole_rows = lax.all_gather(amplitudes, "blk", axis=1, tiled=True)
    owned = lax.all_to_all(whole_rows, "pair", split_axis=1, concat_axis=0, tiled=True)
    hole_rows = hole_ints.shape[0]
    hole_eff = hole_ints * local_mask(hole_mask, blk_index * hole_rows, hole_rows, 0, occupied)
    ladder = jnp.dot(hole_eff, owned, precision=PRECISE)
    return particle + ladder


def solution(mesh):
    placed = (P("pair", "blk"), P("blk", "pair"), P(), P("blk", None), P())
    return jax.shard_map(
        per_device, mesh=mesh, in_specs=placed, out_specs=P("blk", "pair"), check_vma=False
    )
```

profile of v0, /device:TPU:1, one launch (start us, length us, event | category | flops | bytes accessed | tf_op | source)
XLA Modules:
  0.0 157.9 jit_solution(10238636172915307327)
XLA Ops:
  6.5 0.0 all-gather.3.cloned.1.call-start
  6.5 0.7 all-gather.3.cloned.1.call-update
  7.3 12.8 %all_gather.7 = f32[4,16384]{1,0:T(4,128)} all-gather(f32[4,4096]{1,0:T(4,128)} %param.5), channel_id=1, replica_groups=mesh['pair'=128,'blk'=4] {'blk'}, dimensions={1}, use_global_device_ids=true | all-gather | bytes 327680 | tf_op jit(solution)/shard_map/all_gather | solution.py:40
  20.0 19.9 %all-to-all-start = ((f32[4,128,128]{2,0,1:T(4,128)}), f32[4,128,128]{2,0,1:T(4,128)S(1)}, u32[]{:S(2)}, u32[]{:S(2)}) async-start(f32[4,128,128]{2,0,1:T(4,128)} %bitcast.2), calls=%async_computation.1 | async-start | bytes 524288 | tf_op jit(solution)/shard_map/all_to_all | solution.py:41
  39.9 0.0 reduce-scatter.2.cloned.1.call-start
  40.0 1.1 fusion.3
  41.1 4.5 %convolution_multiply_fusion = f32[4096,128]{1,0:T(8,128)S(1)} fusion(f32[4096,128]{1,0:T(8,128)} %param.6, f32[128,128]{1,0:T(8,128)S(1)} %fusion.3, s32[4096]{0:T(1024)S(1)} %add_select_fusion), kind=kOutput, calls=%fused_computation | convolution fusion | flops 806354944 | bytes 4276224 | tf_op jit(solution)/shard_map/dot_general | solution.py:23
  45.6 61.4 %all-gather.3.cloned.1.call-done = f32[128,4,4096]{2,1,0:T(4,128)} async-done(((f32[1,4,4096]{2,1,0:T(4,128)}), f32[128,4,4096]{2,1,0:T(4,128)}) %all-gather.3.cloned.1.call-update) | async-done | bytes 8388624 | tf_op jit(solution)/shard_map/all_gather | solution.py:37
  106.9 10.0 %reshape.152 = f32[512,4096]{1,0:T(8,128)} reshape(f32[128,4,4096]{2,1,0:T(4,128)} %all-gather.3.cloned.1.call-done) | data formatting | bytes 16777216
  116.9 0.0 copy-start.1
  116.9 0.0 copy-start
  116.9 11.8 %convolution_bitcast_fusion = f32[512,128]{0,1:T(8,128)} fusion(f32[4096,128]{1,0:T(8,128)S(1)} %convolution_multiply_fusion, f32[512,4096]{1,0:T(8,128)} %reshape.152), kind=kOutput, calls=%fused_computation.2 | convolution fusion | flops 3221225472 | bytes 10747904 | tf_op jit(solution)/shard_map/dot_general | solution.py:36
  128.7 0.0 reduce-scatter.2.cloned.1.call-update
  128.8 0.0 copy-done.1
  128.8 0.3 fusion.1
  129.1 0.0 copy-done
  129.1 0.3 convolution_multiply_fusion.1
  129.4 0.0 all-to-all-done
  129.5 19.5 %reduce-scatter.2.cloned.1.call-done = f32[128,128]{0,1:T(8,128)} async-done(((f32[512,128]{0,1:T(8,128)}), f32[128,128]{0,1:T(8,128)}) %reduce-scatter.2.cloned.1.call-update) | async-done | bytes 65552 | tf_op jit(solution)/shard_map/reduce_scatter | solution.py:39
  148.9 1.4 convolution_add_fusion
  150.3 0.7 copy.13
  (4 shorter events, 0.0 us)
Async XLA Ops:
  6.5 100.4 %all-gather.3.cloned.1.call-start = ((), (), s32[]{:S(2)}) async-start(), calls=%async_computation.3 | async-start | bytes 8454144 | tf_op jit(solution)/shard_map/all_gather | solution.py:37
  20.0 109.4 %all-to-all-start = ((f32[4,128,128]{2,0,1:T(4,128)}), f32[4,128,128]{2,0,1:T(4,128)S(1)}, u32[]{:S(2)}, u32[]{:S(2)}) async-start(f32[4,128,128]{2,0,1:T(4,128)} %bitcast.2), calls=%async_computation.1 | async-start | bytes 524288 | tf_op jit(solution)/shard_map/all_to_all | solution.py:41
  39.9 109.0 %reduce-scatter.2.cloned.1.call-start = ((), (), s32[]{:S(2)}) async-start(), calls=%async_computation.2 | async-start | bytes 327680 | tf_op jit(solution)/shard_map/reduce_scatter | solution.py:39
  116.9 11.9 %copy-start.1 = (s32[4,4]{1,0:T(4,128)S(1)}, s32[4,4]{1,0:T(4,128)}, u32[]{:S(2)}) copy-start(s32[4,4]{1,0:T(4,128)} %param.9) | copy-start | bytes 196
  116.9 12.2 %copy-start = (f32[128,512]{1,0:T(8,128)S(1)}, f32[128,512]{1,0:T(8,128)}, u32[]{:S(2)}) copy-start(f32[128,512]{1,0:T(8,128)} %param.8) | copy-start | bytes 786436
Sparse Core Ops, SparseCore 0:
  10.5 96.3 all-gather.2
  128.9 19.9 reduce-scatter.1
where the time goes:
time: 160 us; the launch traced here: 158 us
  waiting for transfers between devices  81.6 us (51%)
  starting transfers between devices  19.9 us (12%)
  matrix products  19.4 us (12%)
  between operations  13.5 us (8%)
  blocking collectives  12.8 us (8%)
  local copies, waits for them, and re-layouts  10.7 us (7%)
    all_gather x1, waiting for transfers between devices, per_device(): lax.all_gather(amplitudes, 'pair', axis=0, tiled=True)  61.4 us
    all_to_all x1, starting transfers between devices, per_device(): lax.all_to_all(whole_rows, 'pair', split_axis=1, concat_axis=0, tiled=True)  19.9 us
    reduce_scatter x1, waiting for transfers between devices, per_device(): particle = lax.psum_scatter(product, 'blk', scatter_dimension=0, tiled=True)  19.5 us
    all_gather x1, blocking collectives, per_device(): whole_rows = lax.all_gather(amplitudes, 'blk', axis=1, tiled=True)  12.8 us
    dot_general x1, matrix products, per_device(): jnp.dot(lax.all_gather(amplitudes, 'pair', axis=0, tiled=True), virt_eff,...  11.8 us
    unnamed x5, local copies, waits for them, and re-layouts  9.99 us
    dot_general x2, matrix products, local_mask(): return jnp.dot(rows_pick, inner, precision=PRECISE)  4.77 us
  transfers between devices with their start and end apart: 3, of which 2 were waited for; matrix products, arithmetic and copies ran while one was open for 18% of the time, Pallas kernels for 0%

commit v1 on v0

v1 whole, which is shorter than its diff:
```python
import jax
import jax.numpy as jnp
from jax import lax
from jax.experimental import pallas as pl
from jax.experimental.pallas import tpu as pltpu
from jax.sharding import Mesh
from jax.sharding import PartitionSpec as P

BS = 128
PRECISE = lax.Precision.HIGHEST
PLANE = ("z", "y", "c")
SLOTS = 8


def pair_of(z, y, c):
    return z * 16 + y * 2 + c


FIRST = [[pair_of(z, y, 0) for z in range(8)] for y in range(8)] + [
    [pair_of(z, y, 1) for y in range(8)] for z in range(8)
]
SECOND = [[pair_of(z, y, 0) for y in range(8)] for z in range(8)] + [
    [pair_of(z, y, 1) for z in range(8)] for y in range(8)
]


def halves(low, high):
    rows = lax.broadcasted_iota(jnp.int32, (8, BS), 0)
    return jnp.where(rows < 4, low, high)


def swap(tile):
    return pltpu.roll(tile, 4, 0)


def pack_kernel(pos, slots, held, out, turned):
    c, z, y = pos[0], pos[1], pos[2]
    dest = pl.program_id(0)

    @pl.when(dest == 0)
    def _():
        def turn(two, _):
            for t in range(4):
                a, b = held[2 * t, two], held[2 * t + 1, two]
                turned[2 * two, t] = halves(a, swap(b))
                turned[2 * two + 1, t] = halves(swap(a), b)
            return 0

        lax.fori_loop(0, 16, turn, 0)

    own = jnp.where(c == 0, z * 16 + dest * 2, dest * 16 + y * 2 + 1)
    other = own + 1 - 2 * c
    for s in range(SLOTS):
        out[0, s] = turned[slots[s, own]]
        out[0, SLOTS + s] = turned[slots[s, other]]
    out[0, 2 * SLOTS] = turned[own % 32]
    out[0, 2 * SLOTS + 1] = turned[other % 32]


def pack(pos, slots, held):
    count = 2 * SLOTS + 2
    return pl.pallas_call(
        pack_kernel,
        grid_spec=pltpu.PrefetchScalarGridSpec(
            num_scalar_prefetch=2,
            grid=(8,),
            in_specs=[pl.BlockSpec((8, 16, 8, BS), lambda d, *_: (0, 0, 0, 0))],
            out_specs=pl.BlockSpec((1, count, 4, 8, BS), lambda d, *_: (d, 0, 0, 0, 0)),
            scratch_shapes=[pltpu.VMEM((32, 4, 8, BS), jnp.float32)],
        ),
        out_shape=jax.ShapeDtypeStruct((8, count, 4, 8, BS), jnp.float32),
        name="pack",
    )(pos, slots, held)


def take_kernel(pos, slots, block, out):
    out[0] = block[...]


def take_blocks(pos, slots, virt_ints):
    return pl.pallas_call(
        take_kernel,
        grid_spec=pltpu.PrefetchScalarGridSpec(
            num_scalar_prefetch=2,
            grid=(SLOTS,),
            in_specs=[pl.BlockSpec((BS, BS), lambda s, pos, slots: (slots[s, pos[4]], 0))],
            out_specs=pl.BlockSpec((1, BS, BS), lambda s, *_: (s, 0, 0)),
        ),
        out_shape=jax.ShapeDtypeStruct((SLOTS, BS, BS), jnp.float32),
        name="take",
    )(pos, slots, virt_ints)


def terms_kernel(pos, got, own, other, hole, out, ladder):
    c, z, x = pos[0], pos[1], pos[3]
    active = x == z // 2

    @pl.when(active)
    def _():
        owned = jnp.concatenate(
            [got[:, 2 * SLOTS].reshape(256, BS), got[:, 2 * SLOTS + 1].reshape(256, BS)], axis=1
        )
        for i in range(4):
            ladder[i] = jnp.dot(
                hole[i], owned, precision=PRECISE, preferred_element_type=jnp.float32
            )

    @pl.when(jnp.logical_not(active))
    def _():
        ladder[...] = jnp.zeros_like(ladder)

    for side, blocks in enumerate((own, other)):
        total = jnp.zeros((256, BS), jnp.float32)
        for s in range(0, SLOTS, 2):
            rows = jnp.concatenate(
                [
                    got[:, side * SLOTS + s].reshape(256, BS),
                    got[:, side * SLOTS + s + 1].reshape(256, BS),
                ],
                axis=1,
            )
            total += jnp.dot(
                rows,
                blocks[pl.ds(s, 2)].reshape(2 * BS, BS),
                precision=PRECISE,
                preferred_element_type=jnp.float32,
            )
        total = total.reshape(8, 4, 8, BS)
        first = jnp.where(side == 0, c, 1 - c) * 4
        none = jnp.zeros((8, BS), jnp.float32)

        def put(low, y, tile, i):
            at = pl.ds((low * 8 + y) * 8, 8)
            out[first + i, at] = tile + ladder[i, at, side * BS : (side + 1) * BS]

        @pl.when(c == 0)
        def _():
            for i in range(4):
                for y in range(8):
                    tile = total[y, i]
                    put(0, y, halves(tile, none), i)
                    put(1, y, halves(swap(tile), none), i)

        @pl.when(c == 1)
        def _():
            for i in range(4):
                for low in range(2):
                    for y in range(8):
                        tile = total[2 * i + low, y // 2]
                        put(low, y, halves(none, tile if y % 2 else swap(tile)), i)


def terms(pos, got, own, other, hole):
    whole = lambda shape: pl.BlockSpec(shape, lambda i, *_: (0,) * len(shape))
    args = (got, own, other, hole)
    return pl.pallas_call(
        terms_kernel,
        grid_spec=pltpu.PrefetchScalarGridSpec(
            num_scalar_prefetch=1,
            grid=(1,),
            in_specs=[whole(a.shape) for a in args],
            out_specs=whole((8, BS, BS)),
            scratch_shapes=[pltpu.VMEM((4, BS, 2 * BS), jnp.float32)],
        ),
        out_shape=jax.ShapeDtypeStruct((8, BS, BS), jnp.float32),
        compiler_params=pltpu.CompilerParams(vmem_limit_bytes=40 * 1024 * 1024),
        name="terms",
    )(pos, *args)


def slots_of(mask, x):
    slab = lax.dynamic_slice(mask, (x * 32, 0), (32, BS))
    ids = jnp.arange(32, dtype=jnp.int32)
    upto = (ids[:, None] >= ids[None, :]).astype(jnp.float32)
    rank = jnp.dot(upto, slab.astype(jnp.float32)).astype(jnp.int32)
    want = jnp.arange(1, SLOTS + 1, dtype=jnp.int32)
    hit = (rank[None] == want[:, None, None]) & (slab[None] == 1)
    return jnp.sum(jnp.where(hit, ids[None, :, None], 0), axis=1, dtype=jnp.int32)


def per_device(amplitudes, virt_ints, virt_mask, hole_ints, hole_mask):
    x, z, y, c = (lax.axis_index(a) for a in ("x", "z", "y", "c"))
    pos = jnp.stack([c, z, y, x, pair_of(z, y, c)]).astype(jnp.int32)
    slots = slots_of(virt_mask, x)

    blocks = amplitudes.reshape(4, 32, BS).transpose(1, 0, 2).reshape(1, 16, 8, BS)
    held = lax.all_to_all(
        jnp.broadcast_to(blocks, (8, 16, 8, BS)), PLANE, 0, 0, tiled=True, axis_index_groups=FIRST
    )

    own = take_blocks(pos, slots, virt_ints)
    other = lax.ppermute(own, "c", [(0, 1), (1, 0)])

    keep = jnp.repeat(lax.dynamic_slice(hole_mask, (x, 0), (1, 4)), BS, axis=1).astype(jnp.float32)
    col = jnp.arange(256, dtype=jnp.int32)
    second, first, r = col // 32, col // 4 % 8, col % 4
    wanted = jnp.where(c == 0, first * 64 + second * 8, second * 64 + first * 8 + 4) + r
    pick = (jnp.arange(512, dtype=jnp.int32)[:, None] == wanted[None, :]).astype(jnp.float32)
    hole_rows = jnp.dot(hole_ints * keep, pick, precision=PRECISE)
    hole = lax.all_gather(hole_rows, "x")

    sent = pack(pos, slots, held).reshape(8, 2 * SLOTS + 2, 32, BS)
    got = lax.all_to_all(sent, PLANE, 0, 0, tiled=True, axis_index_groups=SECOND)
    parts = terms(pos, got, own, other, hole)
    parts = lax.all_to_all(parts, ("c", "x"), 0, 0, tiled=True)
    return jnp.sum(parts, axis=0)


def solution(mesh):
    fine = Mesh(mesh.devices.reshape(8, 8, 2, 4), ("z", "y", "c", "x"))
    placed = (P(PLANE, "x"), P("x", PLANE), P(), P("x", None), P())
    return jax.shard_map(
        per_device, mesh=fine, in_specs=placed, out_specs=P("x", PLANE), check_vma=False
    )
```

time: 160 us -> 93.1 us (0.58)
  waiting for transfers between devices: 81.6 us -> 19 us
  matrix products: 19.4 us -> 1.17 us
  Pallas kernels: 0 us -> 15.4 us
  blocking collectives: 12.8 us -> 27.6 us
  between operations: 13.5 us -> 0.06 us
  local copies, waits for them, and re-layouts: 10.7 us -> 4.26 us
  other arithmetic: 0.05 us -> 2.79 us
  starting transfers between devices: 19.9 us -> 22 us
    all_gather x1 -> x0, waiting for transfers between devices: 61.4 us -> none  [per_device(): lax.all_gather(amplitudes, 'pair', axis=0, tiled=True)]
    reduce_scatter x1 -> x0, waiting for transfers between devices: 19.5 us -> none  [per_device(): particle = lax.psum_scatter(product, 'blk', scatter_dimension=0, tiled=True)]
    all_to_all x1 -> x2, waiting for transfers between devices: 0.01 us -> 19 us  [the longest x1 9.71 us: per_device(): lax.all_to_all(sent, PLANE, 0, 0, tiled=True, axis_index_groups=SECOND)]
    dot_general x6 -> x2, matrix products: 19.4 us -> 1.17 us  [the longest x1 0.84 us: slots_of(): rank = jnp.dot(upto, slab.astype(jnp.float32)).astype(jnp.int32)]
    all_to_all x0 -> x1, blocking collectives: none -> 16.2 us  [per_device(): parts = lax.all_to_all(parts, ('c', 'x'), 0, 0, tiled=True)]
    pallas_call x0 -> x3, Pallas kernels: none -> 15.4 us  [the longest x1 5.58 us: take_blocks(): pl.pallas_call(take_kernel, grid_spec=pltpu.PrefetchScalarGridSpec(num_sc...]
    unnamed x5 -> x9, local copies, waits for them, and re-layouts: 9.99 us -> 2.69 us
    ppermute x0 -> x1, starting transfers between devices: none -> 4.28 us  [per_device(): other = lax.ppermute(own, 'c', [(0, 1), (1, 0)])]
  transfers between devices with their start and end apart: 3 -> 3, of which waited for: 2 -> 2; matrix products, arithmetic and copies ran while one was open for 18% -> 4% of each run, Pallas kernels for 0% -> 6%
where the time goes in v1:
time: 93.1 us; the launch traced here: 92.2 us
  blocking collectives  27.6 us (30%)
  starting transfers between devices  22 us (24%)
  waiting for transfers between devices  19 us (20%)
  Pallas kernels  15.4 us (17%)
  local copies, waits for them, and re-layouts  4.26 us (5%)
  other arithmetic  2.79 us (3%)
  matrix products  1.17 us (1%)
    all_to_all x1, blocking collectives, per_device(): parts = lax.all_to_all(parts, ('c', 'x'), 0, 0, tiled=True)  16.2 us
    all_gather x1, blocking collectives, per_device(): hole = lax.all_gather(hole_rows, 'x')  11.4 us
    all_to_all x1, starting transfers between devices, per_device(): lax.all_to_all(sent, PLANE, 0, 0, tiled=True, axis_index_groups=SECOND)  10 us
    all_to_all x1, waiting for transfers between devices, per_device(): lax.all_to_all(sent, PLANE, 0, 0, tiled=True, axis_index_groups=SECOND)  9.71 us
    all_to_all x1, waiting for transfers between devices, per_device(): lax.all_to_all(jnp.broadcast_to(blocks, (8, 16, 8, BS)), PLANE, 0, 0, til...  9.25 us
    all_to_all x1, starting transfers between devices, per_device(): lax.all_to_all(jnp.broadcast_to(blocks, (8, 16, 8, BS)), PLANE, 0, 0, til...  7.65 us
    pallas_call x1, Pallas kernels, take_blocks(): pl.pallas_call(take_kernel, grid_spec=pltpu.PrefetchScalarGridSpec(num_sc...  5.58 us
    pallas_call x1, Pallas kernels, pack(): pl.pallas_call(pack_kernel, grid_spec=pltpu.PrefetchScalarGridSpec(num_sc...  5.03 us
  transfers between devices with their start and end apart: 3, of which 2 were waited for; matrix products, arithmetic and copies ran while one was open for 4% of the time, Pallas kernels for 6%

profile of v1, /device:TPU:1, one launch (start us, length us, event | category | flops | bytes accessed | tf_op | source)
XLA Modules:
  0.0 92.2 jit_solution(6169541133460915087)
XLA Ops:
  0.0 0.8 copy.10
  0.9 0.8 broadcast_in_dim.33
  1.7 7.7 %all-to-all-start = ((f32[8,16,8,128]{3,2,1,0:T(8,128)}), f32[8,16,8,128]{3,2,1,0:T(8,128)S(1)}, u32[]{:S(2)}, u32[]{:S(2)}) async-start(f32[8,16,8,128]{3,2,1,0:T(8,128)} %broadcast_in_dim.33), calls=%async_computation | async-start | bytes 1048576 | tf_op jit(solution)/shard_map/all_to_all | solution.py:187
  9.4 0.6 stack.23.pos
  10.0 0.7 dynamic-slice_compare_fusion
  10.7 0.8 convolution_convert_fusion
  11.6 0.7 select_reduce_fusion.slots
  12.3 9.2 %all-to-all-done.held = f32[8,16,8,128]{3,2,1,0:T(8,128)S(1)} async-done(((f32[8,16,8,128]{3,2,1,0:T(8,128)}), f32[8,16,8,128]{3,2,1,0:T(8,128)S(1)}, u32[]{:S(2)}, u32[]{:S(2)}) %all-to-all-start) | async-done | bytes 524320 | tf_op jit(solution)/shard_map/all_to_all | solution.py:187
  21.5 0.8 copy-done.2
  22.3 5.0 %pack.1 = f32[8,18,4,8,128]{4,3,2,1,0:T(8,128)} custom-call(s32[5]{0:T(128)} %stack.23.pos, s32[8,128]{1,0:T(8,128)} %select_reduce_fusion.slots, f32[8,16,8,128]{3,2,1,0:T(8,128)} %copy-done.2), custom_call_target="tpu_custom_call" | custom-call | tf_op jit(solution)/shard_map/pack/pallas_call | solution.py:62
  27.3 10.0 %all-to-all-start.1 = ((f32[8,18,32,128]{3,2,1,0:T(8,128)}), f32[8,18,32,128]{3,2,1,0:T(8,128)S(1)}, u32[]{:S(2)}, u32[]{:S(2)}) async-start(f32[8,18,32,128]{3,2,1,0:T(8,128)} %bitcast.20), calls=%async_computation.1 | async-start | bytes 4718592 | tf_op jit(solution)/shard_map/all_to_all | solution.py:203
  37.4 0.0 copy-start.1
  37.4 5.6 %take.1.own = f32[8,128,128]{2,1,0:T(8,128)} custom-call(s32[5]{0:T(128)} %stack.23.pos, s32[8,128]{1,0:T(8,128)} %select_reduce_fusion.slots, f32[4096,128]{1,0:T(8,128)} %block.1), custom_call_target="tpu_custom_call" | custom-call | tf_op jit(solution)/shard_map/take/pallas_call | solution.py:81
  43.0 4.3 %collective-permute-start = (f32[8,128,128]{2,1,0:T(8,128)}, f32[8,128,128]{2,1,0:T(8,128)S(1)}, u32[]{:S(2)}, u32[]{:S(2)}) collective-permute-start(f32[8,128,128]{2,1,0:T(8,128)} %take.1.own), channel_id=1, source_target_pairs={{0,4},{4,0},{1,5},{5,1},{2,6},{6,2},{3,7},{7,3},{8,12},{12,8},{9,1... | collective-permute-start | bytes 1572872 | tf_op jit(solution)/shard_map/ppermute | solution.py:192
  47.3 0.7 convert_bitcast_fusion
  48.0 0.1 broadcast_bitcast_fusion
  48.0 0.3 fusion
  48.4 11.4 %all-gather = f32[512,256]{1,0:T(8,128)S(1)} all-gather(f32[128,256]{1,0:T(8,128)S(1)} %fusion), channel_id=2, replica_groups=mesh['z'=8,'y'=8,'c'=2,'x'=4] {'x'}, dimensions={0}, use_global_device_ids=true | all-gather | bytes 655360 | tf_op jit(solution)/shard_map/all_gather | solution.py:200
  59.8 0.0 collective-permute-done.other
  59.8 9.7 %all-to-all-done.1.got = f32[8,18,32,128]{3,2,1,0:T(8,128)S(1)} async-done(((f32[8,18,32,128]{3,2,1,0:T(8,128)}), f32[8,18,32,128]{3,2,1,0:T(8,128)S(1)}, u32[]{:S(2)}, u32[]{:S(2)}) %all-to-all-start.1) | async-done | bytes 2359328 | tf_op jit(solution)/shard_map/all_to_all | solution.py:203
  69.5 1.0 %copy-done = f32[8,128,128]{2,1,0:T(8,128)S(1)} copy-done((f32[8,128,128]{2,1,0:T(8,128)S(1)}, f32[8,128,128]{2,1,0:T(8,128)}, u32[]{:S(2)}) %copy-start) | copy-done | bytes 524312
  70.6 4.8 %terms.1 = f32[8,128,128]{2,1,0:T(8,128)S(1)} custom-call(s32[5]{0:T(128)S(1)} %copy-done.1, f32[8,18,32,128]{3,2,1,0:T(8,128)S(1)} %all-to-all-done.1.got, f32[8,128,128]{2,1,0:T(8,128)S(1)} %copy-done, f32[8,128,128]{2,1,0:T(8,128)S(1)} %collective-permute-done.other, f32[4,128,256]{2,1,0:T(8,128)S(1)} %bitcast.19), custom_call_target="tpu_custom_call" | custom-call | tf_op jit(solution)/shard_map/terms/pallas_call | solution.py:156
  75.3 16.2 %all_to_all.15 = f32[8,128,128]{2,1,0:T(8,128)S(1)} all-to-all(f32[8,128,128]{2,1,0:T(8,128)S(1)} %terms.1), channel_id=1, replica_groups=mesh['z'=8,'y'=8,'c'=2,'x'=4] {'c','x'}, dimensions={0} | all-to-all | bytes 1048576 | tf_op jit(solution)/shard_map/all_to_all | solution.py:205
  91.5 0.7 reduce_sum.19
  (8 shorter events, 0.1 us)
Async XLA Ops:
  1.7 19.8 %all-to-all-start = ((f32[8,16,8,128]{3,2,1,0:T(8,128)}), f32[8,16,8,128]{3,2,1,0:T(8,128)S(1)}, u32[]{:S(2)}, u32[]{:S(2)}) async-start(f32[8,16,8,128]{3,2,1,0:T(8,128)} %broadcast_in_dim.33), calls=%async_computation | async-start | bytes 1048576 | tf_op jit(solution)/shard_map/all_to_all | solution.py:187
  21.5 0.8 copy-start.2
  27.3 42.2 %all-to-all-start.1 = ((f32[8,18,32,128]{3,2,1,0:T(8,128)}), f32[8,18,32,128]{3,2,1,0:T(8,128)S(1)}, u32[]{:S(2)}, u32[]{:S(2)}) async-start(f32[8,18,32,128]{3,2,1,0:T(8,128)} %bitcast.20), calls=%async_computation.1 | async-start | bytes 4718592 | tf_op jit(solution)/shard_map/all_to_all | solution.py:203
  37.4 10.7 %copy-start.3 = (f32[128,512]{1,0:T(8,128)S(1)}, f32[128,512]{1,0:T(8,128)}, u32[]{:S(2)}) copy-start(f32[128,512]{1,0:T(8,128)} %param.8) | copy-start | bytes 786436
  37.4 32.1 %copy-start.1 = (s32[5]{0:T(128)S(1)}, s32[5]{0:T(128)}, u32[]{:S(2)}) copy-start(s32[5]{0:T(128)} %stack.23.pos) | copy-start | bytes 64
  43.0 16.8 %collective-permute-start = (f32[8,128,128]{2,1,0:T(8,128)}, f32[8,128,128]{2,1,0:T(8,128)S(1)}, u32[]{:S(2)}, u32[]{:S(2)}) collective-permute-start(f32[8,128,128]{2,1,0:T(8,128)} %take.1.own), channel_id=1, source_target_pairs={{0,4},{4,0},{1,5},{5,1},{2,6},{6,2},{3,7},{7,3},{8,12},{12,8},{9,1... | collective-permute-start | bytes 1572872 | tf_op jit(solution)/shard_map/ppermute | solution.py:192
  69.5 1.0 %copy-start = (f32[8,128,128]{2,1,0:T(8,128)S(1)}, f32[8,128,128]{2,1,0:T(8,128)}, u32[]{:S(2)}) copy-start(f32[8,128,128]{2,1,0:T(8,128)} %take.1.own) | copy-start | bytes 1572868

commit v2 on v1

v2 whole, which is shorter than its diff:
```python
import jax
import jax.numpy as jnp
from jax import lax
from jax.experimental import pallas as pl
from jax.experimental.pallas import tpu as pltpu
from jax.sharding import Mesh
from jax.sharding import PartitionSpec as P

BS = 128
PLANE = ("z", "y", "c")
SLOTS = 8
MIB = 1024 * 1024
VMEM = pl.BlockSpec(memory_space=pltpu.VMEM)
SMEM = pl.BlockSpec(memory_space=pltpu.SMEM)


def pair_of(z, y, c):
    return z * 16 + y * 2 + c


FIRST = [[pair_of(z, y, 0) for z in range(8)] for y in range(8)] + [
    [pair_of(z, y, 1) for y in range(8)] for z in range(8)
]
SECOND = [[pair_of(z, y, 0) for y in range(8)] for z in range(8)] + [
    [pair_of(z, y, 1) for z in range(8)] for y in range(8)
]


def places():
    return tuple(lax.axis_index(a) for a in ("x", "z", "y", "c"))


def call(kernel, args, out, name, in_specs=None, scratch=(), limit=16):
    return pl.pallas_call(
        kernel,
        in_specs=in_specs or [VMEM] * len(args),
        out_specs=VMEM,
        out_shape=jax.ShapeDtypeStruct(out, jnp.float32),
        scratch_shapes=list(scratch),
        compiler_params=pltpu.CompilerParams(vmem_limit_bytes=limit * MIB),
        name=name,
    )(*args)


def halves(low, high):
    rows = lax.broadcasted_iota(jnp.int32, (8, BS), 0)
    return jnp.where(rows < 4, low, high)


def swap(tile):
    return pltpu.roll(tile, 4, 0)


def pack_kernel(slots, held, out, turned):
    x, z, y, c = places()
    dest = pl.program_id(0)

    @pl.when(dest == 0)
    def _():
        for b in range(32):
            at = slice(b * BS, (b + 1) * BS)
            for t in range(4):
                for h in range(2):
                    turned[b, t, 4 * h : 4 * h + 4] = held[2 * t + h, :, at]

    own = jnp.where(c == 0, z * 16 + dest * 2, dest * 16 + y * 2 + 1)
    other = own + 1 - 2 * c
    for side, column in enumerate((own, other)):
        for s in range(SLOTS):
            out[0, side * SLOTS + s] = turned[slots[s, column]]
        out[0, 2 * SLOTS + side] = turned[column % 32]


def pack(slots, held):
    count = 2 * SLOTS + 2
    return pl.pallas_call(
        pack_kernel,
        grid=(8,),
        in_specs=[SMEM, VMEM],
        out_specs=pl.BlockSpec((1, count, 4, 8, BS), lambda d: (d, 0, 0, 0, 0)),
        out_shape=jax.ShapeDtypeStruct((8, count, 4, 8, BS), jnp.float32),
        scratch_shapes=[pltpu.VMEM((32, 4, 8, BS), jnp.float32)],
        compiler_params=pltpu.CompilerParams(vmem_limit_bytes=16 * MIB),
        name="pack",
    )(slots, held)


def take_kernel(slots, ints, out, sems):
    x, z, y, c = places()
    mine = pair_of(z, y, c)
    copies = []
    for s in range(SLOTS):
        rows = pl.ds(pl.multiple_of(slots[s, mine] * BS, BS), BS)
        copies.append(pltpu.make_async_copy(ints.at[rows], out.at[s], sems.at[s]))
        copies[-1].start()
    for copy in copies:
        copy.wait()


def take(slots, ints):
    return call(
        take_kernel,
        (slots, ints),
        (SLOTS, BS, BS),
        "take",
        in_specs=[SMEM, pl.BlockSpec(memory_space=pl.ANY)],
        scratch=[pltpu.SemaphoreType.DMA((SLOTS,))],
        limit=4,
    )


def parted(value):
    high = value.astype(jnp.bfloat16)
    return high, (value - high.astype(jnp.float32)).astype(jnp.bfloat16)


def product(left, right):
    dot = lambda a, b: jnp.dot(a, b, preferred_element_type=jnp.float32)
    (a, b), (p, q) = parted(left), parted(right)
    return dot(a, p) + (dot(a, q) + dot(b, p))


def terms_kernel(got, own, other, hole, out):
    x, z, y, c = places()
    active = x == z // 2
    firsts = (c * 4, 4 - c * 4)
    column = lambda at: got[:, at].reshape(256, BS)

    @pl.when(active)
    def _():
        owned = jnp.concatenate([column(2 * SLOTS), column(2 * SLOTS + 1)], axis=1)
        for i in range(4):
            ladder = product(hole[i], owned)
            for side in range(2):
                out[firsts[side] + i] = ladder[:, side * BS : (side + 1) * BS]

    @pl.when(jnp.logical_not(active))
    def _():
        out[...] = jnp.zeros_like(out)

    for side, blocks in enumerate((own, other)):
        total = jnp.zeros((256, BS), jnp.float32)
        for s in range(0, SLOTS, 2):
            at = side * SLOTS + s
            rows = jnp.concatenate([column(at), column(at + 1)], axis=1)
            total += product(rows, blocks[s : s + 2].reshape(2 * BS, BS))
        total = total.reshape(8, 4, 8, BS)
        none = jnp.zeros((8, BS), jnp.float32)

        def put(i, low, row, tile, side=side):
            at = slice((low * 8 + row) * 8, (low * 8 + row) * 8 + 8)
            out[firsts[side] + i, at] += tile

        @pl.when(c == 0)
        def _():
            for i in range(4):
                for row in range(8):
                    tile = total[row, i]
                    put(i, 0, row, halves(tile, none))
                    put(i, 1, row, halves(swap(tile), none))

        @pl.when(c == 1)
        def _():
            for i in range(4):
                for low in range(2):
                    for row in range(8):
                        tile = total[2 * i + low, row // 2]
                        put(i, low, row, halves(none, tile if row % 2 else swap(tile)))


def slots_of(mask, x):
    slab = lax.dynamic_slice(mask, (x * 32, 0), (32, BS))
    ids = jnp.arange(32, dtype=jnp.int32)
    upto = (ids[:, None] >= ids[None, :]).astype(jnp.float32)
    rank = jnp.dot(upto, slab.astype(jnp.float32)).astype(jnp.int32)
    want = jnp.arange(1, SLOTS + 1, dtype=jnp.int32)
    hit = (rank[None] == want[:, None, None]) & (slab[None] == 1)
    return jnp.sum(jnp.where(hit, ids[None, :, None], 0), axis=1, dtype=jnp.int32)


def per_device(amplitudes, virt_ints, virt_mask, hole_ints, hole_mask):
    x, z, y, c = places()
    held = lax.all_to_all(
        jnp.broadcast_to(amplitudes[None], (8, 4, 32 * BS)),
        PLANE, 0, 0, tiled=True, axis_index_groups=FIRST,
    )
    slots = slots_of(virt_mask, x)
    own = take(slots, virt_ints)
    other = lax.ppermute(own, "c", [(0, 1), (1, 0)])
    held, own = lax.optimization_barrier((held, own))

    keep = jnp.repeat(lax.dynamic_slice(hole_mask, (x, 0), (1, 4)), BS, axis=1).astype(jnp.float32)
    col = jnp.arange(256, dtype=jnp.int32)
    second, first, r = col // 32, col // 4 % 8, col % 4
    wanted = jnp.where(c == 0, first * 64 + second * 8, second * 64 + first * 8 + 4) + r
    pick = (jnp.arange(512, dtype=jnp.int32)[:, None] == wanted[None, :]).astype(jnp.float32)
    hole_rows = jnp.dot(hole_ints * keep, pick, precision=lax.Precision.HIGHEST)
    hole = lax.all_gather(hole_rows, "x")

    got = lax.all_to_all(
        pack(slots, held), PLANE, 0, 0, tiled=True, axis_index_groups=SECOND
    )
    parts = call(terms_kernel, (got, own, other, hole), (8, BS, BS), "terms")
    parts = lax.all_to_all(parts, ("c", "x"), 0, 0, tiled=True)
    return jnp.sum(parts, axis=0)


def solution(mesh):
    fine = Mesh(mesh.devices.reshape(8, 8, 2, 4), ("z", "y", "c", "x"))
    placed = (P(PLANE, "x"), P("x", PLANE), P(), P("x", None), P())
    return jax.shard_map(
        per_device, mesh=fine, in_specs=placed, out_specs=P("x", PLANE), check_vma=False
    )
```

time: 93.1 us -> 86.8 us (0.932)
  Pallas kernels: 15.4 us -> 5.24 us
  waiting for transfers between devices: 19 us -> 22.7 us
    pallas_call x3, Pallas kernels: 15.4 us -> 5.24 us  [the longest x2 4.03 us: call(): pl.pallas_call(kernel, in_specs=in_specs or [VMEM] * len(args), out_specs...]
    all_to_all x2, waiting for transfers between devices: 19 us -> 22.7 us  [the longest x1 15.3 us: per_device(): lax.all_to_all(pack(slots, held), PLANE, 0, 0, tiled=True, axis_index_gro...]
    unnamed x9 -> x6, local copies, waits for them, and re-layouts: 2.69 us -> 3 us
  transfers between devices with their start and end apart: 3 -> 3, of which waited for: 2 -> 2; matrix products, arithmetic and copies ran while one was open for 4% -> 3% of each run, Pallas kernels for 6% -> 2%
where the time goes in v2:
time: 86.8 us; the launch traced here: 86.2 us
  blocking collectives  27.9 us (32%)
  waiting for transfers between devices  22.7 us (26%)
  starting transfers between devices  22.1 us (25%)
  Pallas kernels  5.24 us (6%)
  local copies, waits for them, and re-layouts  4.77 us (5%)
  other arithmetic  2.2 us (3%)
  matrix products  1.17 us (1%)
    all_to_all x1, blocking collectives, per_device(): parts = lax.all_to_all(parts, ('c', 'x'), 0, 0, tiled=True)  16.4 us
    all_to_all x1, waiting for transfers between devices, per_device(): lax.all_to_all(pack(slots, held), PLANE, 0, 0, tiled=True, axis_index_gro...  15.3 us
    all_gather x1, blocking collectives, per_device(): hole = lax.all_gather(hole_rows, 'x')  11.4 us
    all_to_all x1, starting transfers between devices, per_device(): lax.all_to_all(pack(slots, held), PLANE, 0, 0, tiled=True, axis_index_gro...  10.2 us
    all_to_all x1, starting transfers between devices, per_device(): lax.all_to_all(jnp.broadcast_to(amplitudes[None], (8, 4, 32 * BS)), PLANE...  7.65 us
    all_to_all x1, waiting for transfers between devices, per_device(): lax.all_to_all(jnp.broadcast_to(amplitudes[None], (8, 4, 32 * BS)), PLANE...  7.44 us
    ppermute x1, starting transfers between devices, per_device(): other = lax.ppermute(own, 'c', [(0, 1), (1, 0)])  4.28 us
    pallas_call x2, Pallas kernels, call(): pl.pallas_call(kernel, in_specs=in_specs or [VMEM] * len(args), out_specs...  4.03 us
  transfers between devices with their start and end apart: 3, of which 2 were waited for; matrix products, arithmetic and copies ran while one was open for 3% of the time, Pallas kernels for 2%

profile of v2, /device:TPU:1, one launch (start us, length us, event | category | flops | bytes accessed | tf_op | source)
XLA Modules:
  0.0 86.2 jit_solution(17338529427690537528)
XLA Ops:
  0.0 1.7 %broadcast_in_dim.18 = f32[8,4,4096]{2,1,0:T(4,128)} broadcast(f32[4,4096]{1,0:T(4,128)} %param.5), dimensions={1,2} | broadcast | bytes 589824 | tf_op jit(solution)/shard_map/broadcast_in_dim | solution.py:184
  1.7 7.7 %all-to-all-start = ((f32[8,4,4096]{2,1,0:T(4,128)}), f32[8,4,4096]{2,1,0:T(4,128)S(1)}, u32[]{:S(2)}, u32[]{:S(2)}) async-start(f32[8,4,4096]{2,1,0:T(4,128)} %broadcast_in_dim.18), calls=%async_computation | async-start | bytes 1048576 | tf_op jit(solution)/shard_map/all_to_all | solution.py:183
  9.4 0.7 dynamic-slice_compare_fusion
  10.1 0.8 convolution_convert_fusion
  10.9 0.1 select_reduce_fusion.slots
  11.0 0.0 copy-start.1
  11.1 1.6 %copy-done.1 = f32[4096,128]{1,0:T(8,128)S(1)} copy-done((f32[4096,128]{1,0:T(8,128)S(1)}, f32[4096,128]{1,0:T(8,128)}, u32[]{:S(2)}) %copy-start.1) | copy-done | bytes 2097176
  12.6 1.4 %take.1.own = f32[8,128,128]{2,1,0:T(8,128)S(1)} custom-call(s32[8,128]{1,0:T(8,128)S(1)} %select_reduce_fusion.slots, f32[4096,128]{1,0:T(8,128)S(1)} %copy-done.1), custom_call_target="tpu_custom_call" | custom-call | tf_op jit(solution)/shard_map/take/pallas_call | solution.py:34
  14.1 7.4 %all-to-all-done.held = f32[8,4,4096]{2,1,0:T(4,128)S(1)} async-done(((f32[8,4,4096]{2,1,0:T(4,128)}), f32[8,4,4096]{2,1,0:T(4,128)S(1)}, u32[]{:S(2)}, u32[]{:S(2)}) %all-to-all-start) | async-done | bytes 524320 | tf_op jit(solution)/shard_map/all_to_all | solution.py:183
  21.5 1.2 %pack.1 = f32[8,18,4,8,128]{4,3,2,1,0:T(8,128)S(1)} custom-call(s32[8,128]{1,0:T(8,128)S(1)} %select_reduce_fusion.slots, f32[8,4,4096]{2,1,0:T(4,128)S(1)} %all-to-all-done.held), custom_call_target="tpu_custom_call" | custom-call | tf_op jit(solution)/shard_map/pack/pallas_call | solution.py:76
  22.7 0.0 copy-start
  22.7 1.4 %copy-done = f32[8,18,4,8,128]{4,3,2,1,0:T(8,128)} copy-done((f32[8,18,4,8,128]{4,3,2,1,0:T(8,128)}, f32[8,18,4,8,128]{4,3,2,1,0:T(8,128)S(1)}, u32[]{:S(2)}) %copy-start) | copy-done | bytes 2359320
  24.1 10.2 %all-to-all-start.1 = ((f32[8,18,4,8,128]{4,3,2,1,0:T(8,128)}), f32[8,18,4,8,128]{4,3,2,1,0:T(8,128)S(1)}, u32[]{:S(2)}, u32[]{:S(2)}) async-start(f32[8,18,4,8,128]{4,3,2,1,0:T(8,128)} %copy-done), calls=%async_computation.1 | async-start | bytes 4718592 | tf_op jit(solution)/shard_map/all_to_all | solution.py:200
  34.3 4.3 %collective-permute-start = (f32[8,128,128]{2,1,0:T(8,128)S(1)}, f32[8,128,128]{2,1,0:T(8,128)}, u32[]{:S(2)}, u32[]{:S(2)}) collective-permute-start(f32[8,128,128]{2,1,0:T(8,128)S(1)} %take.1.own), channel_id=1, source_target_pairs={{0,4},{4,0},{1,5},{5,1},{2,6},{6,2},{3,7},{7,3},{8,12},{12,8},{9,1... | collective-permute-start | bytes 1572872 | tf_op jit(solution)/shard_map/ppermute | solution.py:189
  38.6 0.7 convert_bitcast_fusion
  39.3 0.1 broadcast_bitcast_fusion
  39.4 0.0 copy-done.2
  39.4 0.3 fusion
  39.7 11.4 %all-gather = f32[512,256]{1,0:T(8,128)S(1)} all-gather(f32[128,256]{1,0:T(8,128)S(1)} %fusion), channel_id=2, replica_groups=mesh['z'=8,'y'=8,'c'=2,'x'=4] {'x'}, dimensions={0}, use_global_device_ids=true | all-gather | bytes 655360 | tf_op jit(solution)/shard_map/all_gather | solution.py:198
  51.2 0.0 collective-permute-done.other
  51.2 15.3 %all-to-all-done.1.got = f32[8,18,4,8,128]{4,3,2,1,0:T(8,128)S(1)} async-done(((f32[8,18,4,8,128]{4,3,2,1,0:T(8,128)}), f32[8,18,4,8,128]{4,3,2,1,0:T(8,128)S(1)}, u32[]{:S(2)}, u32[]{:S(2)}) %all-to-all-start.1) | async-done | bytes 2359328 | tf_op jit(solution)/shard_map/all_to_all | solution.py:200
  66.5 2.6 %terms.1 = f32[8,128,128]{2,1,0:T(8,128)S(1)} custom-call(f32[8,18,4,8,128]{4,3,2,1,0:T(8,128)S(1)} %all-to-all-done.1.got, f32[8,128,128]{2,1,0:T(8,128)S(1)} %take.1.own, f32[8,128,128]{2,1,0:T(8,128)} %collective-permute-done.other, f32[4,128,256]{2,1,0:T(8,128)S(1)} %bitcast.5), custom_call_target="tpu_custom_call" | custom-call | tf_op jit(solution)/shard_map/terms/pallas_call | solution.py:34
  69.1 16.4 %all_to_all.15 = f32[8,128,128]{2,1,0:T(8,128)S(1)} all-to-all(f32[8,128,128]{2,1,0:T(8,128)S(1)} %terms.1), channel_id=1, replica_groups=mesh['z'=8,'y'=8,'c'=2,'x'=4] {'c','x'}, dimensions={0} | all-to-all | bytes 1048576 | tf_op jit(solution)/shard_map/all_to_all | solution.py:204
  85.5 0.7 reduce_sum.19
  (3 shorter events, 0.0 us)
Async XLA Ops:
  1.7 19.8 %all-to-all-start = ((f32[8,4,4096]{2,1,0:T(4,128)}), f32[8,4,4096]{2,1,0:T(4,128)S(1)}, u32[]{:S(2)}, u32[]{:S(2)}) async-start(f32[8,4,4096]{2,1,0:T(4,128)} %broadcast_in_dim.18), calls=%async_computation | async-start | bytes 1048576 | tf_op jit(solution)/shard_map/all_to_all | solution.py:183
  11.0 1.6 %copy-start.1 = (f32[4096,128]{1,0:T(8,128)S(1)}, f32[4096,128]{1,0:T(8,128)}, u32[]{:S(2)}) copy-start(f32[4096,128]{1,0:T(8,128)} %ints.1) | copy-start | bytes 6291460
  22.7 1.4 %copy-start = (f32[8,18,4,8,128]{4,3,2,1,0:T(8,128)}, f32[8,18,4,8,128]{4,3,2,1,0:T(8,128)S(1)}, u32[]{:S(2)}) copy-start(f32[8,18,4,8,128]{4,3,2,1,0:T(8,128)S(1)} %pack.1) | copy-start | bytes 7077892
  24.1 15.2 %copy-start.2 = (f32[128,512]{1,0:T(8,128)S(1)}, f32[128,512]{1,0:T(8,128)}, u32[]{:S(2)}) copy-start(f32[128,512]{1,0:T(8,128)} %param.8) | copy-start | bytes 786436
  24.1 42.3 %all-to-all-start.1 = ((f32[8,18,4,8,128]{4,3,2,1,0:T(8,128)}), f32[8,18,4,8,128]{4,3,2,1,0:T(8,128)S(1)}, u32[]{:S(2)}, u32[]{:S(2)}) async-start(f32[8,18,4,8,128]{4,3,2,1,0:T(8,128)} %copy-done), calls=%async_computation.1 | async-start | bytes 4718592 | tf_op jit(solution)/shard_map/all_to_all | solution.py:200
  34.3 16.8 %collective-permute-start = (f32[8,128,128]{2,1,0:T(8,128)S(1)}, f32[8,128,128]{2,1,0:T(8,128)}, u32[]{:S(2)}, u32[]{:S(2)}) collective-permute-start(f32[8,128,128]{2,1,0:T(8,128)S(1)} %take.1.own), channel_id=1, source_target_pairs={{0,4},{4,0},{1,5},{5,1},{2,6},{6,2},{3,7},{7,3},{8,12},{12,8},{9,1... | collective-permute-start | bytes 1572872 | tf_op jit(solution)/shard_map/ppermute | solution.py:189

commit v3 on v2

v3 whole, which is shorter than its diff:
```python
import jax
import jax.numpy as jnp
from jax import lax
from jax.experimental import pallas as pl
from jax.experimental.pallas import tpu as pltpu
from jax.sharding import Mesh
from jax.sharding import PartitionSpec as P

BS = 128
PLANE = ("z", "y", "c")
SLOTS = 8
MIB = 1024 * 1024
VMEM = pl.BlockSpec(memory_space=pltpu.VMEM)
SMEM = pl.BlockSpec(memory_space=pltpu.SMEM)
HBM = pl.BlockSpec(memory_space=pltpu.HBM)


def pair_of(z, y, c):
    return z * 16 + y * 2 + c


FIRST = [[pair_of(z, y, 0) for z in range(8)] for y in range(8)] + [
    [pair_of(z, y, 1) for y in range(8)] for z in range(8)
]
SECOND = [[pair_of(z, y, 0) for y in range(8)] for z in range(8)] + [
    [pair_of(z, y, 1) for z in range(8)] for y in range(8)
]


def places():
    return tuple(lax.axis_index(a) for a in ("x", "z", "y", "c"))


def call(kernel, args, out, name, in_specs=None, out_specs=VMEM, scratch=(), limit=16):
    return pl.pallas_call(
        kernel,
        in_specs=in_specs or [VMEM] * len(args),
        out_specs=out_specs,
        out_shape=jax.ShapeDtypeStruct(out, jnp.float32),
        scratch_shapes=list(scratch),
        compiler_params=pltpu.CompilerParams(vmem_limit_bytes=limit * MIB),
        name=name,
    )(*args)


def halves(low, high):
    rows = lax.broadcasted_iota(jnp.int32, (8, BS), 0)
    return jnp.where(rows < 4, low, high)


def swap(tile):
    return pltpu.roll(tile, 4, 0)


def spread_kernel(held, out, sems):
    copies = [pltpu.make_async_copy(held, out.at[k], sems.at[k]) for k in range(8)]
    for copy in copies:
        copy.start()
    for copy in copies:
        copy.wait()


def spread(held):
    return call(
        spread_kernel,
        (held,),
        (8,) + held.shape,
        "spread",
        in_specs=[HBM],
        out_specs=HBM,
        scratch=[pltpu.SemaphoreType.DMA((8,))],
        limit=60,
    )


def pack_kernel(slots, held, out, turned, ready, sems):
    x, z, y, c = places()
    for b in range(32):
        at = slice(b * BS, (b + 1) * BS)
        for t in range(4):
            for h in range(2):
                turned[b, t, 4 * h : 4 * h + 4] = held[2 * t + h, :, at]

    def copy(dest):
        return pltpu.make_async_copy(ready.at[dest], out.at[dest], sems.at[dest])

    def send(dest, _):
        own = jnp.where(c == 0, z * 16 + dest * 2, dest * 16 + y * 2 + 1)
        other = own + 1 - 2 * c
        for side, column in enumerate((own, other)):
            for s in range(SLOTS):
                ready[dest, side * SLOTS + s] = turned[slots[s, column]]
            ready[dest, 2 * SLOTS + side] = turned[column % 32]
        copy(dest).start()
        return 0

    lax.fori_loop(0, 8, send, 0)
    for dest in range(8):
        copy(dest).wait()


def pack(slots, held):
    shape = (8, 2 * SLOTS + 2, 4, 8, BS)
    return call(
        pack_kernel,
        (slots, held),
        shape,
        "pack",
        in_specs=[SMEM, VMEM],
        out_specs=HBM,
        scratch=[
            pltpu.VMEM((32, 4, 8, BS), jnp.float32),
            pltpu.VMEM(shape, jnp.float32),
            pltpu.SemaphoreType.DMA((8,)),
        ],
        limit=58,
    )


def take_kernel(slots, ints, out, sems):
    x, z, y, c = places()
    mine = pair_of(z, y, c)
    copies = []
    for s in range(SLOTS):
        rows = pl.ds(pl.multiple_of(slots[s, mine] * BS, BS), BS)
        copies.append(pltpu.make_async_copy(ints.at[rows], out.at[s], sems.at[s]))
        copies[-1].start()
    for copy in copies:
        copy.wait()


def take(slots, ints):
    return call(
        take_kernel,
        (slots, ints),
        (SLOTS, BS, BS),
        "take",
        in_specs=[SMEM, HBM],
        scratch=[pltpu.SemaphoreType.DMA((SLOTS,))],
        limit=59,
    )


def parted(value):
    high = value.astype(jnp.bfloat16)
    return high, (value - high.astype(jnp.float32)).astype(jnp.bfloat16)


def product(left, right):
    dot = lambda a, b: jnp.dot(a, b, preferred_element_type=jnp.float32)
    (a, b), (p, q) = parted(left), parted(right)
    return dot(a, p) + (dot(a, q) + dot(b, p))


def terms_kernel(side, got, blocks, hole, out):
    x, z, y, c = places()
    active = x == z // 2
    column = lambda at: got[:, at].reshape(256, BS)

    @pl.when(active)
    def _():
        ladder = product(hole[...].reshape(4 * BS, 2 * BS), column(2 * SLOTS + side))
        out[...] = ladder.reshape(4, BS, BS)

    @pl.when(jnp.logical_not(active))
    def _():
        out[...] = jnp.zeros_like(out)

    total = jnp.zeros((256, BS), jnp.float32)
    for s in range(0, SLOTS, 2):
        at = side * SLOTS + s
        rows = jnp.concatenate([column(at), column(at + 1)], axis=1)
        total += product(rows, blocks[s : s + 2].reshape(2 * BS, BS))
    total = total.reshape(8, 4, 8, BS)
    none = jnp.zeros((8, BS), jnp.float32)

    def put(i, low, row, tile):
        at = slice((low * 8 + row) * 8, (low * 8 + row) * 8 + 8)
        out[i, at] += tile

    @pl.when(c == 0)
    def _():
        for i in range(4):
            for row in range(8):
                tile = total[row, i]
                put(i, 0, row, halves(tile, none))
                put(i, 1, row, halves(swap(tile), none))

    @pl.when(c == 1)
    def _():
        for i in range(4):
            for low in range(2):
                for row in range(8):
                    tile = total[2 * i + low, row // 2]
                    put(i, low, row, halves(none, tile if row % 2 else swap(tile)))


def terms(side, got, blocks, hole):
    return call(
        lambda *refs: terms_kernel(side, *refs),
        (got, blocks, hole),
        (4, BS, BS),
        "other_terms" if side else "own_terms",
    )


def slots_of(mask, x):
    slab = lax.dynamic_slice(mask, (x * 32, 0), (32, BS))
    ids = jnp.arange(32, dtype=jnp.int32)
    upto = (ids[:, None] >= ids[None, :]).astype(jnp.float32)
    rank = jnp.dot(upto, slab.astype(jnp.float32)).astype(jnp.int32)
    want = jnp.arange(1, SLOTS + 1, dtype=jnp.int32)
    hit = (rank[None] == want[:, None, None]) & (slab[None] == 1)
    return jnp.sum(jnp.where(hit, ids[None, :, None], 0), axis=1, dtype=jnp.int32)


def per_device(amplitudes, virt_ints, virt_mask, hole_ints, hole_mask):
    x, z, y, c = places()
    held = lax.all_to_all(
        spread(amplitudes),
        PLANE, 0, 0, tiled=True, axis_index_groups=FIRST,
    )
    slots = slots_of(virt_mask, x)
    own = take(slots, virt_ints)
    other = lax.ppermute(own, "c", [(0, 1), (1, 0)])
    held, own = lax.optimization_barrier((held, own))

    keep = jnp.repeat(lax.dynamic_slice(hole_mask, (x, 0), (1, 4)), BS, axis=1).astype(jnp.float32)
    col = jnp.arange(256, dtype=jnp.int32)
    second, first, r = col // 32, col // 4 % 8, col % 4
    wanted = jnp.where(c == 0, first * 64 + second * 8, second * 64 + first * 8 + 4) + r
    pick = (jnp.arange(512, dtype=jnp.int32)[:, None] == wanted[None, :]).astype(jnp.float32)
    hole_rows = jnp.dot(hole_ints * keep, pick, precision=lax.Precision.HIGHEST)
    hole = lax.all_gather(hole_rows, "x")

    got = lax.all_to_all(
        pack(slots, held), PLANE, 0, 0, tiled=True, axis_index_groups=SECOND
    )
    theirs = terms(1, got, other, hole)
    mine = terms(0, got, own, hole)
    parts = mine + lax.ppermute(theirs, "c", [(0, 1), (1, 0)])
    return jnp.sum(lax.all_to_all(parts, "x", 0, 0, tiled=True), axis=0)


def solution(mesh):
    fine = Mesh(mesh.devices.reshape(8, 8, 2, 4), ("z", "y", "c", "x"))
    placed = (P(PLANE, "x"), P("x", PLANE), P(), P("x", None), P())
    return jax.shard_map(
        per_device, mesh=fine, in_specs=placed, out_specs=P("x", PLANE), check_vma=False
    )
```

time: 86.8 us -> 102 us (1.18)
  Pallas kernels: 5.24 us -> 25.4 us
  blocking collectives: 27.9 us -> 20.7 us
  starting transfers between devices: 22.1 us -> 27.4 us
  local copies, waits for them, and re-layouts: 4.77 us -> 0.88 us
    pallas_call x2 -> x5, Pallas kernels: 4.03 us -> 25.4 us  [call(): pl.pallas_call(kernel, in_specs=in_specs or [VMEM] * len(args), out_specs...]
    all_to_all x1, blocking collectives: 16.4 us -> 9.26 us  [per_device(): return jnp.sum(lax.all_to_all(parts, 'x', 0, 0, tiled=True), axis=0)]
    ppermute x0 -> x1, starting transfers between devices: none -> 5.24 us  [per_device(): parts = mine + lax.ppermute(theirs, 'c', [(0, 1), (1, 0)])]
    unnamed x6, local copies, waits for them, and re-layouts: 3 us -> 0.8 us
    broadcast_in_dim x1 -> x0, local copies, waits for them, and re-layouts: 1.7 us -> none  [per_device(): jnp.broadcast_to(amplitudes[None], (8, 4, 32 * BS))]
    pallas_call x1 -> x0, Pallas kernels: 1.22 us -> none  [pack(): pl.pallas_call(pack_kernel, grid=(8,), in_specs=[SMEM, VMEM], out_specs=p...]
  transfers between devices with their start and end apart: 3 -> 4, of which waited for: 2 -> 3; matrix products, arithmetic and copies ran while one was open for 3% -> 3% of each run, Pallas kernels for 2% -> 4%
where the time goes in v3:
time: 102 us; the launch traced here: 101 us
  starting transfers between devices  27.4 us (27%)
  Pallas kernels  25.4 us (25%)
  waiting for transfers between devices  22.6 us (22%)
  blocking collectives  20.7 us (20%)
  other arithmetic  2.81 us (3%)
  matrix products  1.17 us (1%)
    pallas_call x5, Pallas kernels, call(): pl.pallas_call(kernel, in_specs=in_specs or [VMEM] * len(args), out_specs...  25.4 us
    all_to_all x1, waiting for transfers between devices, per_device(): lax.all_to_all(pack(slots, held), PLANE, 0, 0, tiled=True, axis_index_gro...  15.3 us
    all_gather x1, blocking collectives, per_device(): hole = lax.all_gather(hole_rows, 'x')  11.4 us
    all_to_all x1, starting transfers between devices, per_device(): lax.all_to_all(pack(slots, held), PLANE, 0, 0, tiled=True, axis_index_gro...  10.2 us
    all_to_all x1, blocking collectives, per_device(): return jnp.sum(lax.all_to_all(parts, 'x', 0, 0, tiled=True), axis=0)  9.26 us
    all_to_all x1, starting transfers between devices, per_device(): lax.all_to_all(spread(amplitudes), PLANE, 0, 0, tiled=True, axis_index_gr...  7.66 us
    all_to_all x1, waiting for transfers between devices, per_device(): lax.all_to_all(spread(amplitudes), PLANE, 0, 0, tiled=True, axis_index_gr...  7.19 us
    ppermute x1, starting transfers between devices, per_device(): parts = mine + lax.ppermute(theirs, 'c', [(0, 1), (1, 0)])  5.24 us
  transfers between devices with their start and end apart: 4, of which 3 were waited for; matrix products, arithmetic and copies ran while one was open for 3% of the time, Pallas kernels for 4%

profile of v3, /device:TPU:1, one launch (start us, length us, event | category | flops | bytes accessed | tf_op | source)
XLA Modules:
  0.0 101.0 jit_solution(5190165978324602782)
XLA Ops:
  0.0 17.1 %spread.1 = f32[8,4,4096]{2,1,0:T(4,128)} custom-call(f32[4,4096]{1,0:T(4,128)} %held.1), custom_call_target="tpu_custom_call" | custom-call | tf_op jit(solution)/shard_map/spread/pallas_call | solution.py:35
  17.1 7.7 %all-to-all-start = ((f32[8,4,4096]{2,1,0:T(4,128)}), f32[8,4,4096]{2,1,0:T(4,128)S(1)}, u32[]{:S(2)}, u32[]{:S(2)}) async-start(f32[8,4,4096]{2,1,0:T(4,128)} %spread.1), calls=%async_computation | async-start | bytes 1048576 | tf_op jit(solution)/shard_map/all_to_all | solution.py:219
  24.7 0.7 dynamic-slice_compare_fusion
  25.5 0.8 convolution_convert_fusion
  26.3 0.7 select_reduce_fusion.slots
  27.0 2.7 %take.1.refs_1_ = f32[8,128,128]{2,1,0:T(8,128)} custom-call(s32[8,128]{1,0:T(8,128)} %select_reduce_fusion.slots, f32[4096,128]{1,0:T(8,128)} %ints.1), custom_call_target="tpu_custom_call" | custom-call | tf_op jit(solution)/shard_map/take/pallas_call | solution.py:35
  29.7 7.2 %all-to-all-done.held = f32[8,4,4096]{2,1,0:T(4,128)S(1)} async-done(((f32[8,4,4096]{2,1,0:T(4,128)}), f32[8,4,4096]{2,1,0:T(4,128)S(1)}, u32[]{:S(2)}, u32[]{:S(2)}) %all-to-all-start) | async-done | bytes 524320 | tf_op jit(solution)/shard_map/all_to_all | solution.py:219
  36.9 0.8 copy-done.1
  37.7 2.7 %pack.1 = f32[8,18,4,8,128]{4,3,2,1,0:T(8,128)} custom-call(s32[8,128]{1,0:T(8,128)} %select_reduce_fusion.slots, f32[8,4,4096]{2,1,0:T(4,128)} %copy-done.1), custom_call_target="tpu_custom_call" | custom-call | tf_op jit(solution)/shard_map/pack/pallas_call | solution.py:35
  40.3 0.0 copy-start.2
  40.4 10.2 %all-to-all-start.1 = ((f32[8,18,4,8,128]{4,3,2,1,0:T(8,128)}), f32[8,18,4,8,128]{4,3,2,1,0:T(8,128)S(1)}, u32[]{:S(2)}, u32[]{:S(2)}) async-start(f32[8,18,4,8,128]{4,3,2,1,0:T(8,128)} %pack.1), calls=%async_computation.1 | async-start | bytes 4718592 | tf_op jit(solution)/shard_map/all_to_all | solution.py:236
  50.5 4.3 %collective-permute-start = (f32[8,128,128]{2,1,0:T(8,128)S(1)}, f32[8,128,128]{2,1,0:T(8,128)}, u32[]{:S(2)}, u32[]{:S(2)}) collective-permute-start(f32[8,128,128]{2,1,0:T(8,128)S(1)} %copy-done), channel_id=1, source_target_pairs={{0,4},{4,0},{1,5},{5,1},{2,6},{6,2},{3,7},{7,3},{8,12},{12,8},{9,1... | collective-permute-start | bytes 1572872 | tf_op jit(solution)/shard_map/ppermute | solution.py:225
  54.9 0.7 convert_bitcast_fusion
  55.5 0.1 broadcast_bitcast_fusion
  55.6 0.3 fusion
  56.0 11.4 %all-gather = f32[512,256]{1,0:T(8,128)S(1)} all-gather(f32[128,256]{1,0:T(8,128)S(1)} %fusion), channel_id=2, replica_groups=mesh['z'=8,'y'=8,'c'=2,'x'=4] {'x'}, dimensions={0}, use_global_device_ids=true | all-gather | bytes 655360 | tf_op jit(solution)/shard_map/all_gather | solution.py:234
  67.4 0.0 collective-permute-done.refs_1_
  67.4 15.3 %all-to-all-done.1.refs_0_ = f32[8,18,4,8,128]{4,3,2,1,0:T(8,128)S(1)} async-done(((f32[8,18,4,8,128]{4,3,2,1,0:T(8,128)}), f32[8,18,4,8,128]{4,3,2,1,0:T(8,128)S(1)}, u32[]{:S(2)}, u32[]{:S(2)}) %all-to-all-start.1) | async-done | bytes 2359328 | tf_op jit(solution)/shard_map/all_to_all | solution.py:236
  82.7 2.0 %other_terms.1 = f32[4,128,128]{2,1,0:T(8,128)S(1)} custom-call(f32[8,18,4,8,128]{4,3,2,1,0:T(8,128)S(1)} %all-to-all-done.1.refs_0_, f32[8,128,128]{2,1,0:T(8,128)} %collective-permute-done.refs_1_, f32[4,128,256]{2,1,0:T(8,128)S(1)} %bitcast.5), custom_call_target="tpu_custom_call" | custom-call | tf_op jit(solution)/shard_map/other_terms/pallas_call | solution.py:35
  84.7 5.2 %collective-permute-start.1 = (f32[4,128,128]{2,1,0:T(8,128)S(1)}, f32[4,128,128]{2,1,0:T(8,128)S(1)}, u32[]{:S(2)}, u32[]{:S(2)}) collective-permute-start(f32[4,128,128]{2,1,0:T(8,128)S(1)} %other_terms.1), channel_id=1, source_target_pairs={{0,4},{4,0},{1,5},{5,1},{2,6},{6,2},{3,7},{7,3},{8,12},{12,8},{9,1... | collective-permute-start | bytes 786440 | tf_op jit(solution)/shard_map/ppermute | solution.py:241
  89.9 1.0 own_terms.1
  90.9 0.1 collective-permute-done.1
  91.1 9.3 %all_to_all.15 = f32[4,128,128]{2,1,0:T(8,128)S(1)} all-to-all(f32[4,128,128]{2,1,0:T(8,128)S(1)} %add.84), channel_id=1, replica_groups=mesh['z'=8,'y'=8,'c'=2,'x'=4] {'x'}, dimensions={0} | all-to-all | bytes 524288 | tf_op jit(solution)/shard_map/all_to_all | solution.py:242
  100.4 0.6 reduce_sum.19
  (7 shorter events, 0.0 us)
Async XLA Ops:
  17.1 19.8 %all-to-all-start = ((f32[8,4,4096]{2,1,0:T(4,128)}), f32[8,4,4096]{2,1,0:T(4,128)S(1)}, u32[]{:S(2)}, u32[]{:S(2)}) async-start(f32[8,4,4096]{2,1,0:T(4,128)} %spread.1), calls=%async_computation | async-start | bytes 1048576 | tf_op jit(solution)/shard_map/all_to_all | solution.py:219
  36.9 0.8 copy-start.1
  40.3 10.2 %copy-start = (f32[8,128,128]{2,1,0:T(8,128)S(1)}, f32[8,128,128]{2,1,0:T(8,128)}, u32[]{:S(2)}) copy-start(f32[8,128,128]{2,1,0:T(8,128)} %take.1.refs_1_) | copy-start | bytes 1572868
  40.3 15.3 %copy-start.2 = (f32[128,512]{1,0:T(8,128)S(1)}, f32[128,512]{1,0:T(8,128)}, u32[]{:S(2)}) copy-start(f32[128,512]{1,0:T(8,128)} %param.8) | copy-start | bytes 786436
  40.4 42.3 %all-to-all-start.1 = ((f32[8,18,4,8,128]{4,3,2,1,0:T(8,128)}), f32[8,18,4,8,128]{4,3,2,1,0:T(8,128)S(1)}, u32[]{:S(2)}, u32[]{:S(2)}) async-start(f32[8,18,4,8,128]{4,3,2,1,0:T(8,128)} %pack.1), calls=%async_computation.1 | async-start | bytes 4718592 | tf_op jit(solution)/shard_map/all_to_all | solution.py:236
  50.5 16.9 %collective-permute-start = (f32[8,128,128]{2,1,0:T(8,128)S(1)}, f32[8,128,128]{2,1,0:T(8,128)}, u32[]{:S(2)}, u32[]{:S(2)}) collective-permute-start(f32[8,128,128]{2,1,0:T(8,128)S(1)} %copy-done), channel_id=1, source_target_pairs={{0,4},{4,0},{1,5},{5,1},{2,6},{6,2},{3,7},{7,3},{8,12},{12,8},{9,1... | collective-permute-start | bytes 1572872 | tf_op jit(solution)/shard_map/ppermute | solution.py:225
  84.7 6.4 %collective-permute-start.1 = (f32[4,128,128]{2,1,0:T(8,128)S(1)}, f32[4,128,128]{2,1,0:T(8,128)S(1)}, u32[]{:S(2)}, u32[]{:S(2)}) collective-permute-start(f32[4,128,128]{2,1,0:T(8,128)S(1)} %other_terms.1), channel_id=1, source_target_pairs={{0,4},{4,0},{1,5},{5,1},{2,6},{6,2},{3,7},{7,3},{8,12},{12,8},{9,1... | collective-permute-start | bytes 786440 | tf_op jit(solution)/shard_map/ppermute | solution.py:241

commit v4 on v2

--- a/solution.py
+++ b/solution.py
@@ -12,6 +12,7 @@
 MIB = 1024 * 1024
 VMEM = pl.BlockSpec(memory_space=pltpu.VMEM)
 SMEM = pl.BlockSpec(memory_space=pltpu.SMEM)
+HBM = pl.BlockSpec(memory_space=pltpu.HBM)
 
 
 def pair_of(z, y, c):
@@ -30,11 +31,11 @@
     return tuple(lax.axis_index(a) for a in ("x", "z", "y", "c"))
 
 
-def call(kernel, args, out, name, in_specs=None, scratch=(), limit=16):
+def call(kernel, args, out, name, in_specs=None, out_specs=VMEM, scratch=(), limit=16):
     return pl.pallas_call(
         kernel,
         in_specs=in_specs or [VMEM] * len(args),
-        out_specs=VMEM,
+        out_specs=out_specs,
         out_shape=jax.ShapeDtypeStruct(out, jnp.float32),
         scratch_shapes=list(scratch),
         compiler_params=pltpu.CompilerParams(vmem_limit_bytes=limit * MIB),
@@ -51,38 +52,57 @@
     return pltpu.roll(tile, 4, 0)
 
 
-def pack_kernel(slots, held, out, turned):
-    x, z, y, c = places()
-    dest = pl.program_id(0)
-
-    @pl.when(dest == 0)
-    def _():
-        for b in range(32):
-            at = slice(b * BS, (b + 1) * BS)
-            for t in range(4):
-                for h in range(2):
-                    turned[b, t, 4 * h : 4 * h + 4] = held[2 * t + h, :, at]
-
-    own = jnp.where(c == 0, z * 16 + dest * 2, dest * 16 + y * 2 + 1)
-    other = own + 1 - 2 * c
-    for side, column in enumerate((own, other)):
-        for s in range(SLOTS):
-            out[0, side * SLOTS + s] = turned[slots[s, column]]
-        out[0, 2 * SLOTS + side] = turned[column % 32]
+def spread_kernel(held, out):
+    for k in range(8):
+        out[k] = held[...]
+
+
+def spread(held):
+    return call(spread_kernel, (held,), (8,) + held.shape, "spread", limit=60)
+
+
+def pack_kernel(slots, held, out, turned, ready, sems):
+    x, z, y, c = places()
+    for b in range(32):
+        at = slice(b * BS, (b + 1) * BS)
+        for t in range(4):
+            for h in range(2):
+                turned[b, t, 4 * h : 4 * h + 4] = held[2 * t + h, :, at]
+
+    def copy(dest):
+        return pltpu.make_async_copy(ready.at[dest], out.at[dest], sems.at[dest])
+
+    def send(dest, _):
+        own = jnp.where(c == 0, z * 16 + dest * 2, dest * 16 + y * 2 + 1)
+        other = own + 1 - 2 * c
+        for side, column in enumerate((own, other)):
+            for s in range(SLOTS):
+                ready[dest, side * SLOTS + s] = turned[slots[s, column]]
+            ready[dest, 2 * SLOTS + side] = turned[column % 32]
+        copy(dest).start()
+        return 0
+
+    lax.fori_loop(0, 8, send, 0)
+    for dest in range(8):
+        copy(dest).wait()
 
 
 def pack(slots, held):
-    count = 2 * SLOTS + 2
-    return pl.pallas_call(
+    shape = (8, 2 * SLOTS + 2, 4, 8, BS)
+    return call(
         pack_kernel,
-        grid=(8,),
+        (slots, held),
+        shape,
+        "pack",
         in_specs=[SMEM, VMEM],
-        out_specs=pl.BlockSpec((1, count, 4, 8, BS), lambda d: (d, 0, 0, 0, 0)),
-        out_shape=jax.ShapeDtypeStruct((8, count, 4, 8, BS), jnp.float32),
-        scratch_shapes=[pltpu.VMEM((32, 4, 8, BS), jnp.float32)],
-        compiler_params=pltpu.CompilerParams(vmem_limit_bytes=16 * MIB),
-        name="pack",
-    )(slots, held)
+        out_specs=HBM,
+        scratch=[
+            pltpu.VMEM((32, 4, 8, BS), jnp.float32),
+            pltpu.VMEM(shape, jnp.float32),
+            pltpu.SemaphoreType.DMA((8,)),
+        ],
+        limit=52,
+    )
 
 
 def take_kernel(slots, ints, out, sems):
@@ -117,28 +137,32 @@
 def product(left, right):
     dot = lambda a, b: jnp.dot(a, b, preferred_element_type=jnp.float32)
     (a, b), (p, q) = parted(left), parted(right)
-    return dot(a, p) + (dot(a, q) + dot(b, p))
-
-
-def terms_kernel(got, own, other, hole, out):
-    x, z, y, c = places()
+    wide = dot(a, jnp.concatenate([p, q], axis=1))
+    width = right.shape[1]
+    return wide[:, :width] + (wide[:, width:] + dot(b, p))
+
+
+def terms_kernel(got, own, far, hole, out, other, sem):
+    x, z, y, c = places()
+    copy = pltpu.make_async_copy(far, other, sem)
+    copy.start()
     active = x == z // 2
     firsts = (c * 4, 4 - c * 4)
     column = lambda at: got[:, at].reshape(256, BS)
 
     @pl.when(active)
     def _():
-        owned = jnp.concatenate([column(2 * SLOTS), column(2 * SLOTS + 1)], axis=1)
-        for i in range(4):
-            ladder = product(hole[i], owned)
-            for side in range(2):
-                out[firsts[side] + i] = ladder[:, side * BS : (side + 1) * BS]
+        for side in range(2):
+            ladder = product(hole[...].reshape(4 * BS, 2 * BS), column(2 * SLOTS + side))
+            out[pl.ds(firsts[side], 4)] = ladder.reshape(4, BS, BS)
 
     @pl.when(jnp.logical_not(active))
     def _():
         out[...] = jnp.zeros_like(out)
 
     for side, blocks in enumerate((own, other)):
+        if side:
+            copy.wait()
         total = jnp.zeros((256, BS), jnp.float32)
         for s in range(0, SLOTS, 2):
             at = side * SLOTS + s
@@ -181,7 +205,7 @@
 def per_device(amplitudes, virt_ints, virt_mask, hole_ints, hole_mask):
     x, z, y, c = places()
     held = lax.all_to_all(
-        jnp.broadcast_to(amplitudes[None], (8, 4, 32 * BS)),
+        spread(amplitudes),
         PLANE, 0, 0, tiled=True, axis_index_groups=FIRST,
     )
     slots = slots_of(virt_mask, x)
@@ -200,7 +224,14 @@
     got = lax.all_to_all(
         pack(slots, held), PLANE, 0, 0, tiled=True, axis_index_groups=SECOND
     )
-    parts = call(terms_kernel, (got, own, other, hole), (8, BS, BS), "terms")
+    parts = call(
+        terms_kernel,
+        (got, own, other, hole),
+        (8, BS, BS),
+        "terms",
+        in_specs=[VMEM, VMEM, pl.BlockSpec(memory_space=pl.ANY), VMEM],
+        scratch=[pltpu.VMEM((SLOTS, BS, BS), jnp.float32), pltpu.SemaphoreType.DMA],
+    )
     parts = lax.all_to_all(parts, ("c", "x"), 0, 0, tiled=True)
     return jnp.sum(parts, axis=0)
 

time: 86.8 us -> 85.6 us (0.986)
  local copies, waits for them, and re-layouts: 4.77 us -> 1.66 us
  Pallas kernels: 5.24 us -> 6.82 us
    pallas_call x2 -> x4, Pallas kernels: 4.03 us -> 6.82 us  [call(): pl.pallas_call(kernel, in_specs=in_specs or [VMEM] * len(args), out_specs...]
    broadcast_in_dim x1 -> x0, local copies, waits for them, and re-layouts: 1.7 us -> none  [per_device(): jnp.broadcast_to(amplitudes[None], (8, 4, 32 * BS))]
    unnamed x6 -> x4, local copies, waits for them, and re-layouts: 3 us -> 1.59 us
    pallas_call x1 -> x0, Pallas kernels: 1.22 us -> none  [pack(): pl.pallas_call(pack_kernel, grid=(8,), in_specs=[SMEM, VMEM], out_specs=p...]
where the time goes in v4:
time: 85.6 us; the launch traced here: 85 us
  blocking collectives  28.2 us (33%)
  waiting for transfers between devices  22.7 us (27%)
  starting transfers between devices  22.1 us (26%)
  Pallas kernels  6.82 us (8%)
  other arithmetic  2.2 us (3%)
  local copies, waits for them, and re-layouts  1.66 us (2%)
  matrix products  1.17 us (1%)
    all_to_all x1, blocking collectives, per_device(): parts = lax.all_to_all(parts, ('c', 'x'), 0, 0, tiled=True)  16.8 us
    all_to_all x1, waiting for transfers between devices, per_device(): lax.all_to_all(pack(slots, held), PLANE, 0, 0, tiled=True, axis_index_gro...  15.3 us
    all_gather x1, blocking collectives, per_device(): hole = lax.all_gather(hole_rows, 'x')  11.4 us
    all_to_all x1, starting transfers between devices, per_device(): lax.all_to_all(pack(slots, held), PLANE, 0, 0, tiled=True, axis_index_gro...  10.2 us
    all_to_all x1, starting transfers between devices, per_device(): lax.all_to_all(spread(amplitudes), PLANE, 0, 0, tiled=True, axis_index_gr...  7.65 us
    all_to_all x1, waiting for transfers between devices, per_device(): lax.all_to_all(spread(amplitudes), PLANE, 0, 0, tiled=True, axis_index_gr...  7.44 us
    pallas_call x4, Pallas kernels, call(): pl.pallas_call(kernel, in_specs=in_specs or [VMEM] * len(args), out_specs...  6.82 us
    ppermute x1, starting transfers between devices, per_device(): other = lax.ppermute(own, 'c', [(0, 1), (1, 0)])  4.28 us
  transfers between devices with their start and end apart: 3, of which 2 were waited for; matrix products, arithmetic and copies ran while one was open for 3% of the time, Pallas kernels for 2%

profile of v4, /device:TPU:1, one launch (start us, length us, event | category | flops | bytes accessed | tf_op | source)
XLA Modules:
  0.0 85.0 jit_solution(10078429351281579814)
XLA Ops:
  0.0 1.7 %spread.1 = f32[8,4,4096]{2,1,0:T(4,128)} custom-call(f32[4,4096]{1,0:T(4,128)} %held.1), custom_call_target="tpu_custom_call" | custom-call | tf_op jit(solution)/shard_map/spread/pallas_call | solution.py:35
  1.7 7.7 %all-to-all-start = ((f32[8,4,4096]{2,1,0:T(4,128)}), f32[8,4,4096]{2,1,0:T(4,128)S(1)}, u32[]{:S(2)}, u32[]{:S(2)}) async-start(f32[8,4,4096]{2,1,0:T(4,128)} %spread.1), calls=%async_computation | async-start | bytes 1048576 | tf_op jit(solution)/shard_map/all_to_all | solution.py:207
  9.3 0.7 dynamic-slice_compare_fusion
  10.0 0.8 convolution_convert_fusion
  10.9 0.1 select_reduce_fusion.slots
  11.0 0.0 copy-start
  11.0 1.6 %copy-done = f32[4096,128]{1,0:T(8,128)S(1)} copy-done((f32[4096,128]{1,0:T(8,128)S(1)}, f32[4096,128]{1,0:T(8,128)}, u32[]{:S(2)}) %copy-start) | copy-done | bytes 2097176
  12.6 1.4 %take.1.own = f32[8,128,128]{2,1,0:T(8,128)S(1)} custom-call(s32[8,128]{1,0:T(8,128)S(1)} %select_reduce_fusion.slots, f32[4096,128]{1,0:T(8,128)S(1)} %copy-done), custom_call_target="tpu_custom_call" | custom-call | tf_op jit(solution)/shard_map/take/pallas_call | solution.py:35
  14.0 7.4 %all-to-all-done.held = f32[8,4,4096]{2,1,0:T(4,128)S(1)} async-done(((f32[8,4,4096]{2,1,0:T(4,128)}), f32[8,4,4096]{2,1,0:T(4,128)S(1)}, u32[]{:S(2)}, u32[]{:S(2)}) %all-to-all-start) | async-done | bytes 524320 | tf_op jit(solution)/shard_map/all_to_all | solution.py:207
  21.4 2.2 %pack.1 = f32[8,18,4,8,128]{4,3,2,1,0:T(8,128)} custom-call(s32[8,128]{1,0:T(8,128)S(1)} %select_reduce_fusion.slots, f32[8,4,4096]{2,1,0:T(4,128)S(1)} %all-to-all-done.held), custom_call_target="tpu_custom_call" | custom-call | tf_op jit(solution)/shard_map/pack/pallas_call | solution.py:35
  23.7 0.0 copy-start.1
  23.7 10.2 %all-to-all-start.1 = ((f32[8,18,4,8,128]{4,3,2,1,0:T(8,128)}), f32[8,18,4,8,128]{4,3,2,1,0:T(8,128)S(1)}, u32[]{:S(2)}, u32[]{:S(2)}) async-start(f32[8,18,4,8,128]{4,3,2,1,0:T(8,128)} %pack.1), calls=%async_computation.1 | async-start | bytes 4718592 | tf_op jit(solution)/shard_map/all_to_all | solution.py:224
  33.9 4.3 %collective-permute-start = (f32[8,128,128]{2,1,0:T(8,128)S(1)}, f32[8,128,128]{2,1,0:T(8,128)}, u32[]{:S(2)}, u32[]{:S(2)}) collective-permute-start(f32[8,128,128]{2,1,0:T(8,128)S(1)} %take.1.own), channel_id=1, source_target_pairs={{0,4},{4,0},{1,5},{5,1},{2,6},{6,2},{3,7},{7,3},{8,12},{12,8},{9,1... | collective-permute-start | bytes 1572872 | tf_op jit(solution)/shard_map/ppermute | solution.py:213
  38.2 0.7 convert_bitcast_fusion
  38.9 0.1 broadcast_bitcast_fusion
  38.9 0.0 copy-done.1
  38.9 0.3 fusion
  39.3 11.4 %all-gather = f32[512,256]{1,0:T(8,128)S(1)} all-gather(f32[128,256]{1,0:T(8,128)S(1)} %fusion), channel_id=2, replica_groups=mesh['z'=8,'y'=8,'c'=2,'x'=4] {'x'}, dimensions={0}, use_global_device_ids=true | all-gather | bytes 655360 | tf_op jit(solution)/shard_map/all_gather | solution.py:222
  50.7 0.0 collective-permute-done.far
  50.7 15.3 %all-to-all-done.1.got = f32[8,18,4,8,128]{4,3,2,1,0:T(8,128)S(1)} async-done(((f32[8,18,4,8,128]{4,3,2,1,0:T(8,128)}), f32[8,18,4,8,128]{4,3,2,1,0:T(8,128)S(1)}, u32[]{:S(2)}, u32[]{:S(2)}) %all-to-all-start.1) | async-done | bytes 2359328 | tf_op jit(solution)/shard_map/all_to_all | solution.py:224
  66.0 1.5 %terms.1 = f32[8,128,128]{2,1,0:T(8,128)S(1)} custom-call(f32[8,18,4,8,128]{4,3,2,1,0:T(8,128)S(1)} %all-to-all-done.1.got, f32[8,128,128]{2,1,0:T(8,128)S(1)} %take.1.own, f32[8,128,128]{2,1,0:T(8,128)} %collective-permute-done.far, f32[4,128,256]{2,1,0:T(8,128)S(1)} %bitcast.5), custom_call_target="tpu_custom_call" | custom-call | tf_op jit(solution)/shard_map/terms/pallas_call | solution.py:35
  67.6 16.8 %all_to_all.15 = f32[8,128,128]{2,1,0:T(8,128)S(1)} all-to-all(f32[8,128,128]{2,1,0:T(8,128)S(1)} %terms.1), channel_id=1, replica_groups=mesh['z'=8,'y'=8,'c'=2,'x'=4] {'c','x'}, dimensions={0} | all-to-all | bytes 1048576 | tf_op jit(solution)/shard_map/all_to_all | solution.py:235
  84.3 0.7 reduce_sum.19
  (2 shorter events, 0.0 us)
Async XLA Ops:
  1.7 19.8 %all-to-all-start = ((f32[8,4,4096]{2,1,0:T(4,128)}), f32[8,4,4096]{2,1,0:T(4,128)S(1)}, u32[]{:S(2)}, u32[]{:S(2)}) async-start(f32[8,4,4096]{2,1,0:T(4,128)} %spread.1), calls=%async_computation | async-start | bytes 1048576 | tf_op jit(solution)/shard_map/all_to_all | solution.py:207
  11.0 1.6 %copy-start = (f32[4096,128]{1,0:T(8,128)S(1)}, f32[4096,128]{1,0:T(8,128)}, u32[]{:S(2)}) copy-start(f32[4096,128]{1,0:T(8,128)} %ints.1) | copy-start | bytes 6291460
  23.7 15.3 %copy-start.1 = (f32[128,512]{1,0:T(8,128)S(1)}, f32[128,512]{1,0:T(8,128)}, u32[]{:S(2)}) copy-start(f32[128,512]{1,0:T(8,128)} %param.8) | copy-start | bytes 786436
  23.7 42.3 %all-to-all-start.1 = ((f32[8,18,4,8,128]{4,3,2,1,0:T(8,128)}), f32[8,18,4,8,128]{4,3,2,1,0:T(8,128)S(1)}, u32[]{:S(2)}, u32[]{:S(2)}) async-start(f32[8,18,4,8,128]{4,3,2,1,0:T(8,128)} %pack.1), calls=%async_computation.1 | async-start | bytes 4718592 | tf_op jit(solution)/shard_map/all_to_all | solution.py:224
  33.9 16.8 %collective-permute-start = (f32[8,128,128]{2,1,0:T(8,128)S(1)}, f32[8,128,128]{2,1,0:T(8,128)}, u32[]{:S(2)}, u32[]{:S(2)}) collective-permute-start(f32[8,128,128]{2,1,0:T(8,128)S(1)} %take.1.own), channel_id=1, source_target_pairs={{0,4},{4,0},{1,5},{5,1},{2,6},{6,2},{3,7},{7,3},{8,12},{12,8},{9,1... | collective-permute-start | bytes 1572872 | tf_op jit(solution)/shard_map/ppermute | solution.py:213

commit v5 on v4

--- a/solution.py
+++ b/solution.py
@@ -142,24 +142,10 @@
     return wide[:, :width] + (wide[:, width:] + dot(b, p))
 
 
-def terms_kernel(got, own, far, hole, out, other, sem):
-    x, z, y, c = places()
+def particle_kernel(got, own, far, out, other, sem):
     copy = pltpu.make_async_copy(far, other, sem)
     copy.start()
-    active = x == z // 2
-    firsts = (c * 4, 4 - c * 4)
     column = lambda at: got[:, at].reshape(256, BS)
-
-    @pl.when(active)
-    def _():
-        for side in range(2):
-            ladder = product(hole[...].reshape(4 * BS, 2 * BS), column(2 * SLOTS + side))
-            out[pl.ds(firsts[side], 4)] = ladder.reshape(4, BS, BS)
-
-    @pl.when(jnp.logical_not(active))
-    def _():
-        out[...] = jnp.zeros_like(out)
-
     for side, blocks in enumerate((own, other)):
         if side:
             copy.wait()
@@ -168,28 +154,44 @@
             at = side * SLOTS + s
             rows = jnp.concatenate([column(at), column(at + 1)], axis=1)
             total += product(rows, blocks[s : s + 2].reshape(2 * BS, BS))
-        total = total.reshape(8, 4, 8, BS)
-        none = jnp.zeros((8, BS), jnp.float32)
-
-        def put(i, low, row, tile, side=side):
-            at = slice((low * 8 + row) * 8, (low * 8 + row) * 8 + 8)
-            out[firsts[side] + i, at] += tile
+        out[side] = total.reshape(8, 4, 8, BS)
+
+
+def terms_kernel(total, got, swapped, hole, out):
+    x, z, y, c = places()
+    firsts = (c * 4, 4 - c * 4)
+    for side in range(2):
 
         @pl.when(c == 0)
         def _():
             for i in range(4):
-                for row in range(8):
-                    tile = total[row, i]
-                    put(i, 0, row, halves(tile, none))
-                    put(i, 1, row, halves(swap(tile), none))
+                out[firsts[side] + i] = total[side, :, i]
 
         @pl.when(c == 1)
         def _():
             for i in range(4):
-                for low in range(2):
-                    for row in range(8):
-                        tile = total[2 * i + low, row // 2]
-                        put(i, low, row, halves(none, tile if row % 2 else swap(tile)))
+                out[firsts[side] + i] = total[side, 2 * i : 2 * i + 2].reshape(8, 8, BS)
+
+        @pl.when(x == z // 2)
+        def _():
+            rows = jnp.concatenate(
+                [
+                    got[:, 2 * SLOTS + side].reshape(256, BS),
+                    swapped[:, 1 - side].reshape(256, BS),
+                ],
+                axis=0,
+            )
+            ladder = product(hole[...].reshape(256, 512), rows).reshape(4, 8, 8, BS)
+            out[pl.ds(firsts[side], 4)] += ladder
+
+
+def add_kernel(parts, out):
+    a, b = (parts[k] + parts[k + 1] + parts[k + 2] + parts[k + 3] for k in (0, 4))
+    for low in range(2):
+        for row in range(8):
+            u, v = a[row], b[low * 4 + row // 2]
+            at = (low * 8 + row) * 8
+            out[at : at + 8] = halves(swap(u) if low else u, v if row % 2 else swap(v))
 
 
 def slots_of(mask, x):
@@ -214,26 +216,33 @@
     held, own = lax.optimization_barrier((held, own))
 
     keep = jnp.repeat(lax.dynamic_slice(hole_mask, (x, 0), (1, 4)), BS, axis=1).astype(jnp.float32)
-    col = jnp.arange(256, dtype=jnp.int32)
-    second, first, r = col // 32, col // 4 % 8, col % 4
-    wanted = jnp.where(c == 0, first * 64 + second * 8, second * 64 + first * 8 + 4) + r
-    pick = (jnp.arange(512, dtype=jnp.int32)[:, None] == wanted[None, :]).astype(jnp.float32)
-    hole_rows = jnp.dot(hole_ints * keep, pick, precision=lax.Precision.HIGHEST)
-    hole = lax.all_gather(hole_rows, "x")
+    ids = jnp.arange(512, dtype=jnp.int32)
+    second, first, r = ids % 256 // 32, ids // 4 % 8, ids % 4
+    kind = jnp.where(ids < 256, c, 1 - c)
+    wanted = jnp.where(kind == 0, first * 64 + second * 8, second * 64 + first * 8 + 4) + r
+    columns = (ids[:, None] == wanted[None, :]).astype(jnp.float32)
+    row = jnp.arange(64, dtype=jnp.int32)
+    start = jnp.where(c == 0, row // 4 % 2 * 64 + row // 8 * 8, row // 4 * 8 + 4) + row % 4
+    rows = (start[:, None] == ids[None, :BS]).astype(jnp.float32)
+    exact = lambda a, b: jnp.dot(a, b, precision=lax.Precision.HIGHEST)
+    hole = lax.all_gather(exact(exact(rows, hole_ints * keep), columns), "x")
 
     got = lax.all_to_all(
         pack(slots, held), PLANE, 0, 0, tiled=True, axis_index_groups=SECOND
     )
-    parts = call(
-        terms_kernel,
-        (got, own, other, hole),
-        (8, BS, BS),
-        "terms",
-        in_specs=[VMEM, VMEM, pl.BlockSpec(memory_space=pl.ANY), VMEM],
+    got, other, hole = lax.optimization_barrier((got, other, hole))
+    swapped = lax.ppermute(got[:, 2 * SLOTS :], "c", [(0, 1), (1, 0)])
+    total = call(
+        particle_kernel,
+        (got, own, other),
+        (2, 8, 4, 8, BS),
+        "particle",
+        in_specs=[VMEM, VMEM, pl.BlockSpec(memory_space=pl.ANY)],
         scratch=[pltpu.VMEM((SLOTS, BS, BS), jnp.float32), pltpu.SemaphoreType.DMA],
     )
+    parts = call(terms_kernel, (total, got, swapped, hole), (8, 8, 8, BS), "terms")
     parts = lax.all_to_all(parts, ("c", "x"), 0, 0, tiled=True)
-    return jnp.sum(parts, axis=0)
+    return call(add_kernel, (parts,), (BS, BS), "add_terms")
 
 
 def solution(mesh):

time: 85.6 us -> 84.9 us (level)
  blocking collectives: 28.2 us -> 21.6 us
  starting transfers between devices: 22.1 us -> 27.3 us
  Pallas kernels: 6.82 us -> 8.07 us
    all_to_all x1, blocking collectives: 16.8 us -> 10.2 us  [per_device(): parts = lax.all_to_all(parts, ('c', 'x'), 0, 0, tiled=True)]
    ppermute x0 -> x1, starting transfers between devices: none -> 5.24 us  [per_device(): swapped = lax.ppermute(got[:, 2 * SLOTS:], 'c', [(0, 1), (1, 0)])]
    pallas_call x4 -> x6, Pallas kernels: 6.82 us -> 8.07 us  [call(): pl.pallas_call(kernel, in_specs=in_specs or [VMEM] * len(args), out_specs...]
  transfers between devices with their start and end apart: 3 -> 4, of which waited for: 2 -> 2; matrix products, arithmetic and copies ran while one was open for 3% -> 4% of each run, Pallas kernels for 2% -> 3%
where the time goes in v5:
time: 84.9 us; the launch traced here: 84.3 us
  starting transfers between devices  27.3 us (32%)
  waiting for transfers between devices  22.3 us (26%)
  blocking collectives  21.6 us (25%)
  Pallas kernels  8.07 us (10%)
  local copies, waits for them, and re-layouts  1.69 us (2%)
  matrix products  1.58 us (2%)
  other arithmetic  1.56 us (2%)
    all_to_all x1, waiting for transfers between devices, per_device(): lax.all_to_all(pack(slots, held), PLANE, 0, 0, tiled=True, axis_index_gro...  14.8 us
    all_gather x1, blocking collectives, per_device(): hole = lax.all_gather(exact(exact(rows, hole_ints * keep), columns), 'x')  11.4 us
    all_to_all x1, blocking collectives, per_device(): parts = lax.all_to_all(parts, ('c', 'x'), 0, 0, tiled=True)  10.2 us
    all_to_all x1, starting transfers between devices, per_device(): lax.all_to_all(pack(slots, held), PLANE, 0, 0, tiled=True, axis_index_gro...  10.2 us
    pallas_call x6, Pallas kernels, call(): pl.pallas_call(kernel, in_specs=in_specs or [VMEM] * len(args), out_specs...  8.07 us
    all_to_all x1, starting transfers between devices, per_device(): lax.all_to_all(spread(amplitudes), PLANE, 0, 0, tiled=True, axis_index_gr...  7.65 us
    all_to_all x1, waiting for transfers between devices, per_device(): lax.all_to_all(spread(amplitudes), PLANE, 0, 0, tiled=True, axis_index_gr...  7.44 us
    ppermute x1, starting transfers between devices, per_device(): swapped = lax.ppermute(got[:, 2 * SLOTS:], 'c', [(0, 1), (1, 0)])  5.24 us
  transfers between devices with their start and end apart: 4, of which 2 were waited for; matrix products, arithmetic and copies ran while one was open for 4% of the time, Pallas kernels for 3%

profile of v5, /device:TPU:1, one launch (start us, length us, event | category | flops | bytes accessed | tf_op | source)
XLA Modules:
  0.0 84.3 jit_solution(16309061326419583114)
XLA Ops:
  0.0 1.7 %spread.1 = f32[8,4,4096]{2,1,0:T(4,128)} custom-call(f32[4,4096]{1,0:T(4,128)} %held.1), custom_call_target="tpu_custom_call" | custom-call | tf_op jit(solution)/shard_map/spread/pallas_call | solution.py:35
  1.7 7.7 %all-to-all-start = ((f32[8,4,4096]{2,1,0:T(4,128)}), f32[8,4,4096]{2,1,0:T(4,128)S(1)}, u32[]{:S(2)}, u32[]{:S(2)}) async-start(f32[8,4,4096]{2,1,0:T(4,128)} %spread.1), calls=%async_computation | async-start | bytes 1048576 | tf_op jit(solution)/shard_map/all_to_all | solution.py:209
  9.3 0.7 dynamic-slice_compare_fusion
  10.0 0.8 convolution_convert_fusion
  10.9 0.1 select_reduce_fusion.slots
  11.0 0.0 copy-start
  11.0 1.6 %copy-done = f32[4096,128]{1,0:T(8,128)S(1)} copy-done((f32[4096,128]{1,0:T(8,128)S(1)}, f32[4096,128]{1,0:T(8,128)}, u32[]{:S(2)}) %copy-start) | copy-done | bytes 2097176
  12.6 1.4 %take.1.own = f32[8,128,128]{2,1,0:T(8,128)S(1)} custom-call(s32[8,128]{1,0:T(8,128)S(1)} %select_reduce_fusion.slots, f32[4096,128]{1,0:T(8,128)S(1)} %copy-done), custom_call_target="tpu_custom_call" | custom-call | tf_op jit(solution)/shard_map/take/pallas_call | solution.py:35
  14.0 7.4 %all-to-all-done.held = f32[8,4,4096]{2,1,0:T(4,128)S(1)} async-done(((f32[8,4,4096]{2,1,0:T(4,128)}), f32[8,4,4096]{2,1,0:T(4,128)S(1)}, u32[]{:S(2)}, u32[]{:S(2)}) %all-to-all-start) | async-done | bytes 524320 | tf_op jit(solution)/shard_map/all_to_all | solution.py:209
  21.5 2.2 %pack.1 = f32[8,18,4,8,128]{4,3,2,1,0:T(8,128)} custom-call(s32[8,128]{1,0:T(8,128)S(1)} %select_reduce_fusion.slots, f32[8,4,4096]{2,1,0:T(4,128)S(1)} %all-to-all-done.held), custom_call_target="tpu_custom_call" | custom-call | tf_op jit(solution)/shard_map/pack/pallas_call | solution.py:35
  23.7 0.0 copy-start.1
  23.7 10.2 %all-to-all-start.1 = ((f32[8,18,4,8,128]{4,3,2,1,0:T(8,128)}), f32[8,18,4,8,128]{4,3,2,1,0:T(8,128)S(1)}, u32[]{:S(2)}, u32[]{:S(2)}) async-start(f32[8,18,4,8,128]{4,3,2,1,0:T(8,128)} %pack.1), calls=%async_computation.1 | async-start | bytes 4718592 | tf_op jit(solution)/shard_map/all_to_all | solution.py:230
  33.9 4.3 %collective-permute-start = (f32[8,128,128]{2,1,0:T(8,128)S(1)}, f32[8,128,128]{2,1,0:T(8,128)}, u32[]{:S(2)}, u32[]{:S(2)}) collective-permute-start(f32[8,128,128]{2,1,0:T(8,128)S(1)} %take.1.own), channel_id=1, source_target_pairs={{0,4},{4,0},{1,5},{5,1},{2,6},{6,2},{3,7},{7,3},{8,12},{12,8},{9,1... | collective-permute-start | bytes 1572872 | tf_op jit(solution)/shard_map/ppermute | solution.py:215
  38.2 0.7 convert_bitcast_fusion
  38.9 0.1 broadcast_bitcast_fusion
  39.0 0.3 fusion.2
  39.2 0.5 fusion
  39.7 11.4 %all-gather = f32[256,512]{1,0:T(8,128)S(1)} all-gather(f32[64,512]{1,0:T(8,128)S(1)} %fusion), channel_id=2, replica_groups=mesh['z'=8,'y'=8,'c'=2,'x'=4] {'x'}, dimensions={0}, use_global_device_ids=true | all-gather | bytes 655360 | tf_op jit(solution)/shard_map/all_gather | solution.py:228
  51.2 14.8 %all-to-all-done.1.got = f32[8,18,4,8,128]{4,3,2,1,0:T(8,128)S(1)} async-done(((f32[8,18,4,8,128]{4,3,2,1,0:T(8,128)}), f32[8,18,4,8,128]{4,3,2,1,0:T(8,128)S(1)}, u32[]{:S(2)}, u32[]{:S(2)}) %all-to-all-start.1) | async-done | bytes 2359328 | tf_op jit(solution)/shard_map/all_to_all | solution.py:230
  66.0 5.2 %collective-permute-start.1 = (f32[8,2,4,8,128]{4,3,2,1,0:T(8,128)S(1)}, f32[8,2,4,8,128]{4,3,2,1,0:T(8,128)S(1)}, u32[]{:S(2)}, u32[]{:S(2)}) collective-permute-start(f32[8,2,4,8,128]{4,3,2,1,0:T(8,128)S(1)} %slice.7), channel_id=1, source_target_pairs={{0,4},{4,0},{1,5},{5,1},{2,6},{6,2},{3,7},{7,3},{8,12},{12,8},{9,1... | collective-permute-start | bytes 786440 | tf_op jit(solution)/shard_map/ppermute | solution.py:234
  71.3 1.5 %particle.1.total = f32[2,8,4,8,128]{4,3,2,1,0:T(8,128)S(1)} custom-call(f32[8,18,4,8,128]{4,3,2,1,0:T(8,128)S(1)} %all-to-all-done.1.got, f32[8,128,128]{2,1,0:T(8,128)S(1)} %take.1.own, f32[8,128,128]{2,1,0:T(8,128)} %collective-permute-done.far), custom_call_target="tpu_custom_call" | custom-call | tf_op jit(solution)/shard_map/particle/pallas_call | solution.py:35
  72.8 0.6 terms.1
  73.4 10.2 %all_to_all.15.parts = f32[8,8,8,128]{3,2,1,0:T(8,128)S(1)} all-to-all(f32[8,8,8,128]{3,2,1,0:T(8,128)S(1)} %terms.1), channel_id=1, replica_groups=mesh['z'=8,'y'=8,'c'=2,'x'=4] {'c','x'}, dimensions={0} | all-to-all | bytes 524288 | tf_op jit(solution)/shard_map/all_to_all | solution.py:244
  83.6 0.6 add_terms.1
  (9 shorter events, 0.1 us)
Async XLA Ops:
  1.7 19.8 %all-to-all-start = ((f32[8,4,4096]{2,1,0:T(4,128)}), f32[8,4,4096]{2,1,0:T(4,128)S(1)}, u32[]{:S(2)}, u32[]{:S(2)}) async-start(f32[8,4,4096]{2,1,0:T(4,128)} %spread.1), calls=%async_computation | async-start | bytes 1048576 | tf_op jit(solution)/shard_map/all_to_all | solution.py:209
  11.0 1.6 %copy-start = (f32[4096,128]{1,0:T(8,128)S(1)}, f32[4096,128]{1,0:T(8,128)}, u32[]{:S(2)}) copy-start(f32[4096,128]{1,0:T(8,128)} %ints.1) | copy-start | bytes 6291460
  23.7 15.3 %copy-start.1 = (f32[128,512]{1,0:T(8,128)S(1)}, f32[128,512]{1,0:T(8,128)}, u32[]{:S(2)}) copy-start(f32[128,512]{1,0:T(8,128)} %param.8) | copy-start | bytes 786436
  23.7 42.3 %all-to-all-start.1 = ((f32[8,18,4,8,128]{4,3,2,1,0:T(8,128)}), f32[8,18,4,8,128]{4,3,2,1,0:T(8,128)S(1)}, u32[]{:S(2)}, u32[]{:S(2)}) async-start(f32[8,18,4,8,128]{4,3,2,1,0:T(8,128)} %pack.1), calls=%async_computation.1 | async-start | bytes 4718592 | tf_op jit(solution)/shard_map/all_to_all | solution.py:230
  33.9 17.3 %collective-permute-start = (f32[8,128,128]{2,1,0:T(8,128)S(1)}, f32[8,128,128]{2,1,0:T(8,128)}, u32[]{:S(2)}, u32[]{:S(2)}) collective-permute-start(f32[8,128,128]{2,1,0:T(8,128)S(1)} %take.1.own), channel_id=1, source_target_pairs={{0,4},{4,0},{1,5},{5,1},{2,6},{6,2},{3,7},{7,3},{8,12},{12,8},{9,1... | collective-permute-start | bytes 1572872 | tf_op jit(solution)/shard_map/ppermute | solution.py:215
  66.0 6.8 %collective-permute-start.1 = (f32[8,2,4,8,128]{4,3,2,1,0:T(8,128)S(1)}, f32[8,2,4,8,128]{4,3,2,1,0:T(8,128)S(1)}, u32[]{:S(2)}, u32[]{:S(2)}) collective-permute-start(f32[8,2,4,8,128]{4,3,2,1,0:T(8,128)S(1)} %slice.7), channel_id=1, source_target_pairs={{0,4},{4,0},{1,5},{5,1},{2,6},{6,2},{3,7},{7,3},{8,12},{12,8},{9,1... | collective-permute-start | bytes 786440 | tf_op jit(solution)/shard_map/ppermute | solution.py:234

commit v6 on v5

--- a/solution.py
+++ b/solution.py
@@ -142,35 +142,56 @@
     return wide[:, :width] + (wide[:, width:] + dot(b, p))
 
 
-def particle_kernel(got, own, far, out, other, sem):
-    copy = pltpu.make_async_copy(far, other, sem)
-    copy.start()
+def split_kernel(own, other, rows, own_out, other_out, rows_out):
+    rows_out[...] = rows[...]
+    for blocks, out in ((own, own_out), (other, other_out)):
+        for s in range(0, SLOTS, 2):
+            high, low = parted(blocks[s : s + 2].reshape(2 * BS, BS))
+            out[s // 2] = jnp.concatenate([high, low], axis=1)
+
+
+def split(own, other, rows):
+    wide = jax.ShapeDtypeStruct((SLOTS // 2, 2 * BS, 2 * BS), jnp.bfloat16)
+    return pl.pallas_call(
+        split_kernel,
+        in_specs=[VMEM] * 3,
+        out_specs=[VMEM] * 3,
+        out_shape=[wide, wide, jax.ShapeDtypeStruct(rows.shape, rows.dtype)],
+        compiler_params=pltpu.CompilerParams(vmem_limit_bytes=16 * MIB),
+        name="split",
+    )(own, other, rows)
+
+
+def particle_kernel(got, own, other, out):
     column = lambda at: got[:, at].reshape(256, BS)
     for side, blocks in enumerate((own, other)):
-        if side:
-            copy.wait()
-        total = jnp.zeros((256, BS), jnp.float32)
+        total = jnp.zeros((512, 2 * BS), jnp.float32)
         for s in range(0, SLOTS, 2):
             at = side * SLOTS + s
             rows = jnp.concatenate([column(at), column(at + 1)], axis=1)
-            total += product(rows, blocks[s : s + 2].reshape(2 * BS, BS))
-        out[side] = total.reshape(8, 4, 8, BS)
+            total += jnp.dot(
+                jnp.concatenate(parted(rows), axis=0),
+                blocks[s // 2],
+                preferred_element_type=jnp.float32,
+            )
+        low = total[256:, :BS] + (total[:256, BS:] + total[256:, BS:])
+        out[side] = (total[:256, :BS] + low).reshape(8, 4, 8, BS)
 
 
 def terms_kernel(total, got, swapped, hole, out):
     x, z, y, c = places()
-    firsts = (c * 4, 4 - c * 4)
+    firsts = (c, 1 - c)
     for side in range(2):
 
         @pl.when(c == 0)
         def _():
             for i in range(4):
-                out[firsts[side] + i] = total[side, :, i]
+                out[firsts[side] + 2 * i] = total[side, :, i]
 
         @pl.when(c == 1)
         def _():
             for i in range(4):
-                out[firsts[side] + i] = total[side, 2 * i : 2 * i + 2].reshape(8, 8, BS)
+                out[firsts[side] + 2 * i] = total[side, 2 * i : 2 * i + 2].reshape(8, 8, BS)
 
         @pl.when(x == z // 2)
         def _():
@@ -182,11 +203,12 @@
                 axis=0,
             )
             ladder = product(hole[...].reshape(256, 512), rows).reshape(4, 8, 8, BS)
-            out[pl.ds(firsts[side], 4)] += ladder
+            for i in range(4):
+                out[firsts[side] + 2 * i] += ladder[i]
 
 
 def add_kernel(parts, out):
-    a, b = (parts[k] + parts[k + 1] + parts[k + 2] + parts[k + 3] for k in (0, 4))
+    a, b = (parts[k] + parts[k + 2] + parts[k + 4] + parts[k + 6] for k in (0, 1))
     for low in range(2):
         for row in range(8):
             u, v = a[row], b[low * 4 + row // 2]
@@ -225,23 +247,18 @@
     start = jnp.where(c == 0, row // 4 % 2 * 64 + row // 8 * 8, row // 4 * 8 + 4) + row % 4
     rows = (start[:, None] == ids[None, :BS]).astype(jnp.float32)
     exact = lambda a, b: jnp.dot(a, b, precision=lax.Precision.HIGHEST)
-    hole = lax.all_gather(exact(exact(rows, hole_ints * keep), columns), "x")
+    hole_rows = exact(exact(rows, hole_ints * keep), columns)
+    own, other, hole_rows = split(own, other, hole_rows)
+    hole = lax.all_gather(hole_rows, "x")
 
     got = lax.all_to_all(
         pack(slots, held), PLANE, 0, 0, tiled=True, axis_index_groups=SECOND
     )
-    got, other, hole = lax.optimization_barrier((got, other, hole))
+    got, hole = lax.optimization_barrier((got, hole))
     swapped = lax.ppermute(got[:, 2 * SLOTS :], "c", [(0, 1), (1, 0)])
-    total = call(
-        particle_kernel,
-        (got, own, other),
-        (2, 8, 4, 8, BS),
-        "particle",
-        in_specs=[VMEM, VMEM, pl.BlockSpec(memory_space=pl.ANY)],
-        scratch=[pltpu.VMEM((SLOTS, BS, BS), jnp.float32), pltpu.SemaphoreType.DMA],
-    )
+    total = call(particle_kernel, (got, own, other), (2, 8, 4, 8, BS), "particle")
     parts = call(terms_kernel, (total, got, swapped, hole), (8, 8, 8, BS), "terms")
-    parts = lax.all_to_all(parts, ("c", "x"), 0, 0, tiled=True)
+    parts = lax.all_to_all(parts, ("x", "c"), 0, 0, tiled=True)
     return call(add_kernel, (parts,), (BS, BS), "add_terms")
 
 

time: 84.9 us -> 85 us (level)
  waiting for transfers between devices: 22.3 us -> 18.6 us
  local copies, waits for them, and re-layouts: 1.69 us -> 5.33 us
  matrix products: 1.58 us -> 2.53 us
    all_to_all x1, waiting for transfers between devices: 14.8 us -> 11.1 us  [per_device(): lax.all_to_all(pack(slots, held), PLANE, 0, 0, tiled=True, axis_index_gro...]
    unnamed x4 -> x10, local copies, waits for them, and re-layouts: 1.59 us -> 5.23 us
    dot_general x2, matrix products: 0.74 us -> 1.69 us  [per_device(): exact = lambda a, b: jnp.dot(a, b, precision=lax.Precision.HIGHEST)]
  transfers between devices with their start and end apart: 4 -> 4, of which waited for: 2 -> 2; matrix products, arithmetic and copies ran while one was open for 4% -> 5% of each run, Pallas kernels for 3% -> 3%
where the time goes in v6:
time: 85 us; the launch traced here: 84.3 us
  starting transfers between devices  27.2 us (32%)
  blocking collectives  21.5 us (25%)
  waiting for transfers between devices  18.6 us (22%)
  Pallas kernels  7.43 us (9%)
  local copies, waits for them, and re-layouts  5.33 us (6%)
  matrix products  2.53 us (3%)
  other arithmetic  1.55 us (2%)
    all_gather x1, blocking collectives, per_device(): hole = lax.all_gather(hole_rows, 'x')  11.4 us
    all_to_all x1, waiting for transfers between devices, per_device(): lax.all_to_all(pack(slots, held), PLANE, 0, 0, tiled=True, axis_index_gro...  11.1 us
    all_to_all x1, blocking collectives, per_device(): parts = lax.all_to_all(parts, ('x', 'c'), 0, 0, tiled=True)  10.1 us
    all_to_all x1, starting transfers between devices, per_device(): lax.all_to_all(pack(slots, held), PLANE, 0, 0, tiled=True, axis_index_gro...  10 us
    all_to_all x1, starting transfers between devices, per_device(): lax.all_to_all(spread(amplitudes), PLANE, 0, 0, tiled=True, axis_index_gr...  7.65 us
    all_to_all x1, waiting for transfers between devices, per_device(): lax.all_to_all(spread(amplitudes), PLANE, 0, 0, tiled=True, axis_index_gr...  7.44 us
    pallas_call x6, Pallas kernels, call(): pl.pallas_call(kernel, in_specs=in_specs or [VMEM] * len(args), out_specs...  7.29 us
    ppermute x1, starting transfers between devices, per_device(): swapped = lax.ppermute(got[:, 2 * SLOTS:], 'c', [(0, 1), (1, 0)])  5.24 us
  transfers between devices with their start and end apart: 4, of which 2 were waited for; matrix products, arithmetic and copies ran while one was open for 5% of the time, Pallas kernels for 3%

profile of v6, /device:TPU:1, one launch (start us, length us, event | category | flops | bytes accessed | tf_op | source)
XLA Modules:
  0.0 84.3 jit_solution(11868853082545825502)
XLA Ops:
  0.0 1.7 %spread.1 = f32[8,4,4096]{2,1,0:T(4,128)} custom-call(f32[4,4096]{1,0:T(4,128)} %held.1), custom_call_target="tpu_custom_call" | custom-call | tf_op jit(solution)/shard_map/spread/pallas_call | solution.py:35
  1.7 7.7 %all-to-all-start = ((f32[8,4,4096]{2,1,0:T(4,128)}), f32[8,4,4096]{2,1,0:T(4,128)S(1)}, u32[]{:S(2)}, u32[]{:S(2)}) async-start(f32[8,4,4096]{2,1,0:T(4,128)} %spread.1), calls=%async_computation | async-start | bytes 1048576 | tf_op jit(solution)/shard_map/all_to_all | solution.py:231
  9.3 0.7 dynamic-slice_compare_fusion
  10.1 0.8 convolution_convert_fusion
  11.0 1.6 %copy-done = f32[4096,128]{1,0:T(8,128)S(1)} copy-done((f32[4096,128]{1,0:T(8,128)S(1)}, f32[4096,128]{1,0:T(8,128)}, u32[]{:S(2)}) %copy-start) | copy-done | bytes 2097176
  12.6 1.4 %take.1.own = f32[8,128,128]{2,1,0:T(8,128)S(1)} custom-call(s32[8,128]{1,0:T(8,128)S(1)} %select_reduce_fusion.slots, f32[4096,128]{1,0:T(8,128)S(1)} %copy-done), custom_call_target="tpu_custom_call" | custom-call | tf_op jit(solution)/shard_map/take/pallas_call | solution.py:35
  14.0 7.4 %all-to-all-done.held = f32[8,4,4096]{2,1,0:T(4,128)S(1)} async-done(((f32[8,4,4096]{2,1,0:T(4,128)}), f32[8,4,4096]{2,1,0:T(4,128)S(1)}, u32[]{:S(2)}, u32[]{:S(2)}) %all-to-all-start) | async-done | bytes 524320 | tf_op jit(solution)/shard_map/all_to_all | solution.py:231
  21.5 2.2 %pack.1 = f32[8,18,4,8,128]{4,3,2,1,0:T(8,128)} custom-call(s32[8,128]{1,0:T(8,128)S(1)} %select_reduce_fusion.slots, f32[8,4,4096]{2,1,0:T(4,128)S(1)} %all-to-all-done.held), custom_call_target="tpu_custom_call" | custom-call | tf_op jit(solution)/shard_map/pack/pallas_call | solution.py:35
  23.7 10.0 %all-to-all-start.1 = ((f32[8,18,4,8,128]{4,3,2,1,0:T(8,128)}), f32[8,18,4,8,128]{4,3,2,1,0:T(8,128)S(1)}, u32[]{:S(2)}, u32[]{:S(2)}) async-start(f32[8,18,4,8,128]{4,3,2,1,0:T(8,128)} %pack.1), calls=%async_computation.1 | async-start | bytes 4718592 | tf_op jit(solution)/shard_map/all_to_all | solution.py:254
  33.7 4.3 %collective-permute-start = (f32[8,128,128]{2,1,0:T(8,128)S(1)}, f32[8,128,128]{2,1,0:T(8,128)S(1)}, u32[]{:S(2)}, u32[]{:S(2)}) collective-permute-start(f32[8,128,128]{2,1,0:T(8,128)S(1)} %take.1.own), channel_id=1, source_target_pairs={{0,4},{4,0},{1,5},{5,1},{2,6},{6,2},{3,7},{7,3},{8,12},{12,8},{9,1... | collective-permute-start | bytes 1572872 | tf_op jit(solution)/shard_map/ppermute | solution.py:237
  38.0 0.7 convert_bitcast_fusion
  38.8 1.2 %fusion.2 = f32[64,512]{1,0:T(8,128)S(1)} fusion(f32[128,512]{1,0:T(8,128)} %param.8, f32[512]{0:T(512)S(1)} %broadcast_bitcast_fusion, s32[128]{0:T(128)S(1)} %slice.6, s32[64]{0:T(128)S(1)} %fusion.26), kind=kOutput, calls=%fused_computation.4 | convolution fusion | flops 50405376 | bytes 396032 | tf_op jit(solution)/shard_map/dot_general | solution.py:249
  40.0 0.5 fusion.rows
  40.6 0.8 copy-done.3
  41.3 1.0 %copy-done.4 = f32[8,128,128]{2,1,0:T(8,128)S(1)} copy-done((f32[8,128,128]{2,1,0:T(8,128)S(1)}, f32[8,128,128]{2,1,0:T(8,128)}, u32[]{:S(2)}) %copy-start.4) | copy-done | bytes 524312
  42.5 0.8 copy-done.1
  43.3 11.4 %all-gather = f32[256,512]{1,0:T(8,128)S(1)} all-gather(f32[64,512]{1,0:T(8,128)S(1)} %get-tuple-element.14), channel_id=2, replica_groups=mesh['z'=8,'y'=8,'c'=2,'x'=4] {'x'}, dimensions={0}, use_global_device_ids=true | all-gather | bytes 655360 | tf_op jit(solution)/shard_map/all_gather | solution.py:252
  54.7 11.1 %all-to-all-done.1.got = f32[8,18,4,8,128]{4,3,2,1,0:T(8,128)S(1)} async-done(((f32[8,18,4,8,128]{4,3,2,1,0:T(8,128)}), f32[8,18,4,8,128]{4,3,2,1,0:T(8,128)S(1)}, u32[]{:S(2)}, u32[]{:S(2)}) %all-to-all-start.1) | async-done | bytes 2359328 | tf_op jit(solution)/shard_map/all_to_all | solution.py:254
  65.9 5.2 %collective-permute-start.1 = (f32[8,2,4,8,128]{4,3,2,1,0:T(8,128)S(1)}, f32[8,2,4,8,128]{4,3,2,1,0:T(8,128)S(1)}, u32[]{:S(2)}, u32[]{:S(2)}) collective-permute-start(f32[8,2,4,8,128]{4,3,2,1,0:T(8,128)S(1)} %slice.7), channel_id=1, source_target_pairs={{0,4},{4,0},{1,5},{5,1},{2,6},{6,2},{3,7},{7,3},{8,12},{12,8},{9,1... | collective-permute-start | bytes 786440 | tf_op jit(solution)/shard_map/ppermute | solution.py:258
  71.2 1.0 %copy-done.2 = bf16[4,256,256]{2,1,0:T(8,128)(2,1)S(1)} copy-done((bf16[4,256,256]{2,1,0:T(8,128)(2,1)S(1)}, bf16[4,256,256]{2,1,0:T(8,128)(2,1)}, u32[]{:S(2)}) %copy-start.2) | copy-done | bytes 524312
  72.2 0.7 particle.1.total
  72.9 0.6 terms.1
  73.6 10.1 %all_to_all.15.parts = f32[8,8,8,128]{3,2,1,0:T(8,128)S(1)} all-to-all(f32[8,8,8,128]{3,2,1,0:T(8,128)S(1)} %terms.1), channel_id=1, replica_groups=mesh['z'=8,'y'=8,'c'=2,'x'=4] {'x','c'}, dimensions={0} | all-to-all | bytes 524288 | tf_op jit(solution)/shard_map/all_to_all | solution.py:261
  83.7 0.6 add_terms.1
  (16 shorter events, 0.4 us)
Async XLA Ops:
  1.7 19.8 %all-to-all-start = ((f32[8,4,4096]{2,1,0:T(4,128)}), f32[8,4,4096]{2,1,0:T(4,128)S(1)}, u32[]{:S(2)}, u32[]{:S(2)}) async-start(f32[8,4,4096]{2,1,0:T(4,128)} %spread.1), calls=%async_computation | async-start | bytes 1048576 | tf_op jit(solution)/shard_map/all_to_all | solution.py:231
  11.0 1.6 %copy-start = (f32[4096,128]{1,0:T(8,128)S(1)}, f32[4096,128]{1,0:T(8,128)}, u32[]{:S(2)}) copy-start(f32[4096,128]{1,0:T(8,128)} %ints.1) | copy-start | bytes 6291460
  23.7 42.2 %all-to-all-start.1 = ((f32[8,18,4,8,128]{4,3,2,1,0:T(8,128)}), f32[8,18,4,8,128]{4,3,2,1,0:T(8,128)S(1)}, u32[]{:S(2)}, u32[]{:S(2)}) async-start(f32[8,18,4,8,128]{4,3,2,1,0:T(8,128)} %pack.1), calls=%async_computation.1 | async-start | bytes 4718592 | tf_op jit(solution)/shard_map/all_to_all | solution.py:254
  33.7 6.8 %collective-permute-start = (f32[8,128,128]{2,1,0:T(8,128)S(1)}, f32[8,128,128]{2,1,0:T(8,128)S(1)}, u32[]{:S(2)}, u32[]{:S(2)}) collective-permute-start(f32[8,128,128]{2,1,0:T(8,128)S(1)} %take.1.own), channel_id=1, source_target_pairs={{0,4},{4,0},{1,5},{5,1},{2,6},{6,2},{3,7},{7,3},{8,12},{12,8},{9,1... | collective-permute-start | bytes 1572872 | tf_op jit(solution)/shard_map/ppermute | solution.py:237
  40.5 0.8 copy-start.3
  41.3 1.0 %copy-start.4 = (f32[8,128,128]{2,1,0:T(8,128)S(1)}, f32[8,128,128]{2,1,0:T(8,128)}, u32[]{:S(2)}) copy-start(f32[8,128,128]{2,1,0:T(8,128)} %copy-done.3) | copy-start | bytes 1572868
  42.5 0.8 copy-start.1
  65.9 7.0 %collective-permute-start.1 = (f32[8,2,4,8,128]{4,3,2,1,0:T(8,128)S(1)}, f32[8,2,4,8,128]{4,3,2,1,0:T(8,128)S(1)}, u32[]{:S(2)}, u32[]{:S(2)}) collective-permute-start(f32[8,2,4,8,128]{4,3,2,1,0:T(8,128)S(1)} %slice.7), channel_id=1, source_target_pairs={{0,4},{4,0},{1,5},{5,1},{2,6},{6,2},{3,7},{7,3},{8,12},{12,8},{9,1... | collective-permute-start | bytes 786440 | tf_op jit(solution)/shard_map/ppermute | solution.py:258
  71.1 1.0 %copy-start.2 = (bf16[4,256,256]{2,1,0:T(8,128)(2,1)S(1)}, bf16[4,256,256]{2,1,0:T(8,128)(2,1)}, u32[]{:S(2)}) copy-start(bf16[4,256,256]{2,1,0:T(8,128)(2,1)} %copy-done.1) | copy-start | bytes 1572868
